TPU v7x, 256 devices: a whole 4x4x8 slice. The times are simulated.
256 devices in a mesh: rep: 16 (over x, z_lo), seq: 16 (over z_hi, y, core).
Axes of the slice: x: 4, y: 4, z: 8 (z_hi: 2, z_lo: 4; z = z_hi * 4 + z_lo), core: 2. Of those that a mesh axis runs over, the one named last changes fastest.
Arguments:
- tokens: bfloat16 [16, 1536, 5120], P('rep', 'seq'), may hold values from -6 to 6
- steps: int32 [16], P('rep'), may hold values from 0 to 49
- counts: int32 [16], P('rep'), may hold values from 768 to 1536, as said below
- mod_base: float32 [2, 5120], replicated, may hold values from -3 to 3
- mod_time: float32 [2, 5120], replicated, may hold values from -3 to 3
- w_query: float32 [5120, 4096], P('rep', 'seq')
- w_key: float32 [5120, 4096], P('rep', 'seq')
- w_value: float32 [5120, 4096], P('rep', 'seq'), may hold values from -0.078125 to 0.078125
Outputs:
- attended: bfloat16 [16, 1536, 4096], P('rep', 'seq')
Inputs may be any that keep to these rules, and one draw needn't show every extreme that they name: Keys at positions counts[r] or later are padding; some replica has all 1536 tokens valid.
All inputs are finite; a program needn't handle non-finite values.
Results may differ from a plain program's by a relative error of at most 0.015.
The roundings to bfloat16 on the way count: a program that leaves them out, or rounds other values in their place, can miss the bound.
Values may be sent and summed in bfloat16 or wider, within the bound.
No kernel may reach another device: no remote copies, remote signals or barrier semaphores. Data moves between devices by JAX's collectives and lax.ppermute only.
A program may use at most 128 MiB of HBM per device.

v0:
```python
import math

import jax
import jax.numpy as jnp
from jax import lax
from jax.sharding import PartitionSpec as P

HEAD = 128
STEPS = 50


def modulation(step_value, mod_base, mod_time, width):
    frac = 1.0 - step_value.astype(jnp.float32) / STEPS
    sigma = 5.0 * frac / (1.0 + 4.0 * frac)
    half_width = width // 2
    freqs = jnp.exp(-math.log(10000.0) * jnp.arange(half_width, dtype=jnp.float32) / half_width)
    angles = 1000.0 * sigma * freqs
    embedding = jnp.concatenate([jnp.cos(angles), jnp.sin(angles)])
    return (mod_base[0] + mod_time[0] * embedding, mod_base[1] + mod_time[1] * embedding)


def modulate(token_rows, shift_row, scale_row):
    values = token_rows.astype(jnp.float32)
    center = jnp.mean(values, axis=1, keepdims=True)
    spread = jnp.mean((values - center) ** 2, axis=1, keepdims=True)
    normed = (values - center) * lax.rsqrt(spread + 1e-06)
    return (normed * (1.0 + scale_row) + shift_row).astype(jnp.bfloat16)


def attend(query, keys, values, valid_count):
    total = query.shape[0]
    head_count = query.shape[1] // HEAD
    block_size = min(512, total)
    query3 = query.reshape(total // block_size, block_size, head_count, HEAD)
    keys3 = keys.reshape(total, head_count, HEAD)
    values3 = values.reshape(total, head_count, HEAD)
    valid = jnp.arange(total) < valid_count

    def one_block(query_block):
        scores = jnp.einsum(
            "qhd,khd->hqk", query_block, keys3, preferred_element_type=jnp.float32
        ) / math.sqrt(HEAD)
        scores = jnp.where(valid[None, None, :], scores, -1e30)
        top = jnp.max(scores, axis=2, keepdims=True)
        weights = jnp.exp(scores - top)
        probs = (weights / jnp.sum(weights, axis=2, keepdims=True)).astype(jnp.bfloat16)
        result = jnp.einsum("hqk,khd->qhd", probs, values3, preferred_element_type=jnp.float32)
        return result.reshape(block_size, head_count * HEAD).astype(jnp.bfloat16)

    return lax.map(one_block, query3).reshape(total, head_count * HEAD)


def shards(tokens, steps, counts, mod_base, mod_time, w_query, w_key, w_value):
    local_rows = tokens[0]
    head_width = w_query.shape[1]
    shift_row, scale_row = modulation(steps[0], mod_base, mod_time, local_rows.shape[1])
    valid_count = counts[0]
    low_weights = (
        w_query.astype(jnp.bfloat16),
        w_key.astype(jnp.bfloat16),
        w_value.astype(jnp.bfloat16),
    )
    source_rows = modulate(local_rows, shift_row, scale_row)
    full_weights = (
        lax.all_gather(low_weights[0], "rep", axis=0, tiled=True),
        lax.all_gather(low_weights[1], "rep", axis=0, tiled=True),
        lax.all_gather(low_weights[2], "rep", axis=0, tiled=True),
    )
    joined = jnp.concatenate(full_weights, axis=1)
    projected = jnp.dot(
        lax.all_gather(source_rows, "seq", axis=0, tiled=True),
        joined,
        preferred_element_type=jnp.float32,
    ).astype(jnp.bfloat16)
    query = projected[:, :head_width]
    keys = projected[:, head_width : 2 * head_width]
    values = projected[:, 2 * head_width :]
    head_output = attend(query, keys, values, valid_count)
    attended = lax.all_to_all(head_output, "seq", split_axis=0, concat_axis=1, tiled=True)
    return attended[None]


def solution(mesh):
    in_specs = (
        P("rep", "seq", None),
        P("rep"),
        P("rep"),
        P(),
        P(),
        P("rep", "seq"),
        P("rep", "seq"),
        P("rep", "seq"),
    )
    out_specs = P("rep", "seq", None)
    return jax.shard_map(shards, mesh=mesh, in_specs=in_specs, out_specs=out_specs, check_vma=False)
```

profile of v0, /device:TPU:2, one launch (start us, length us, event | category | flops | bytes accessed | tf_op | source)
XLA Modules:
  0.0 527.3 jit_solution(16075871136727537037)
XLA Ops:
  6.5 1.6 convert_element_type.50
  8.2 1.7 convert_element_type.48
  10.0 1.7 convert_element_type.49
  12.4 1.4 convert_reduce_fusion
  13.8 1.6 fusion.49
  15.5 0.3 fusion.53
  15.8 0.9 add_add_fusion
  16.8 2.6 fusion.52
  19.4 76.4 %all-gather.11.cloned.1.call-done = bf16[5120,256]{1,0:T(8,128)(2,1)} async-done(((bf16[320,256]{1,0:T(8,128)(2,1)}), bf16[5120,256]{1,0:T(8,128)(2,1)}) %all-gather.11.cloned.1.call-update) | async-done | bytes 2621456 | tf_op jit(solution)/shard_map/all_gather | solution.py:67
  95.7 90.2 %all-gather.7.cloned.1.call-done = bf16[5120,256]{1,0:T(8,128)(2,1)} async-done(((bf16[320,256]{1,0:T(8,128)(2,1)}), bf16[5120,256]{1,0:T(8,128)(2,1)}) %all-gather.7.cloned.1.call-update) | async-done | bytes 2621456 | tf_op jit(solution)/shard_map/all_gather | solution.py:65
  185.9 90.2 %all-gather.9.cloned.1.call-done = bf16[5120,256]{1,0:T(8,128)(2,1)} async-done(((bf16[320,256]{1,0:T(8,128)(2,1)}), bf16[5120,256]{1,0:T(8,128)(2,1)}) %all-gather.9.cloned.1.call-update) | async-done | bytes 2621456 | tf_op jit(solution)/shard_map/all_gather | solution.py:66
  276.1 173.9 %all-gather.5.cloned.1.call-done = bf16[1536,5120]{1,0:T(8,128)(2,1)} async-done(((bf16[96,5120]{1,0:T(8,128)(2,1)}), bf16[1536,5120]{1,0:T(8,128)(2,1)}) %all-gather.5.cloned.1.call-update) | async-done | bytes 15728656 | tf_op jit(solution)/shard_map/all_gather | solution.py:71
  450.0 16.1 %fusion.43 = bf16[1536,768]{0,1:T(8,128)(2,1)S(1)} fusion(bf16[1536,5120]{1,0:T(8,128)(2,1)} %all-gather.5.cloned.1.call-done, bf16[5120,256]{1,0:T(8,128)(2,1)} %all-gather.11.cloned.1.call-done, bf16[5120,256]{1,0:T(8,128)(2,1)} %all-gather.9.cloned.1.call-done, bf16[5120,256]{1,0:T(8,128)(2,1)} %all-gather.7.cloned.1.call-done), kind=kOutput, calls=%fused_computation.33 | convolution fusion | flops 12104368128 | bytes 25952256 | tf_op jit(solution)/shard_map/dot_general | solution.py:70
  466.2 0.6 reshape.78
  466.8 0.8 copy.16
  467.7 1.2 copy.17
  468.8 25.5 %while.11 = (s32[]{:T(128)}, bf16[3,512,256]{2,1,0:T(8,128)(2,1)}, bf16[3,512,2,128]{3,1,2,0:T(8,128)(2,1)S(1)}, bf16[1536,2,128]{2,0,1:T(8,128)(2,1)}, bf16[153...) while((s32[]{:T(128)}, bf16[3,512,256]{2,1,0:T(8,128)(2,1)}, ...), condition=%wide.region_5.6_spmd.clone, body=%wide.region_2.5_spmd.clone.sunk | while | flops 1222252032 | bytes 4208729 | solution.py:50
  468.8 0.7 iota_compare_fusion.2
  469.5 3.2 fusion.76
  472.6 3.8 fusion.77
  476.6 0.7 constant_dynamic-update-slice_fusion.2
  477.3 0.7 iota_compare_fusion.2
  478.0 3.2 fusion.76
  481.1 3.8 fusion.77
  485.1 0.7 constant_dynamic-update-slice_fusion.2
  485.8 0.7 iota_compare_fusion.2
  486.5 3.2 fusion.76
  489.6 3.8 fusion.77
  493.6 0.7 constant_dynamic-update-slice_fusion.2
  494.3 24.9 %all_to_all.16 = bf16[16,96,256]{2,1,0:T(8,128)(2,1)S(1)} all-to-all(bf16[16,96,256]{2,1,0:T(8,128)(2,1)} %bitcast.63), channel_id=1, replica_groups=mesh['rep'=16,'seq'=16] {'seq'}, dimensions={0} | all-to-all | bytes 1572864 | tf_op jit(solution)/shard_map/all_to_all | solution.py:79
  519.1 0.4 copy.19
  519.6 1.2 broadcast_in_dim.28
  (15 shorter events, 0.8 us)
Async XLA Ops:
  6.5 89.2 %all-gather.11.cloned.1.call-start = ((), (), s32[]{:S(2)}) async-start(), calls=%async_computation.4 | async-start | bytes 2785280 | tf_op jit(solution)/shard_map/all_gather | solution.py:67
  8.2 177.7 %all-gather.7.cloned.1.call-start = ((), (), s32[]{:S(2)}) async-start(), calls=%async_computation.2 | async-start | bytes 2785280 | tf_op jit(solution)/shard_map/all_gather | solution.py:65
  9.9 266.2 %all-gather.9.cloned.1.call-start = ((), (), s32[]{:S(2)}) async-start(), calls=%async_computation.3 | async-start | bytes 2785280 | tf_op jit(solution)/shard_map/all_gather | solution.py:66
  11.7 438.3 %all-gather.5.cloned.1.call-start = ((), (), s32[]{:S(2)}) async-start(), calls=%async_computation.1 | async-start | bytes 16711680 | tf_op jit(solution)/shard_map/all_gather | solution.py:71
Sparse Core Ops, SparseCore 0:
  9.1 86.5 all-gather.10
  97.5 88.3 all-gather.6
  187.7 88.3 all-gather.8
  278.7 171.2 all-gather.4
where the time goes:
time: 530 us; the launch traced here: 527 us
  waiting for transfers between devices  431 us (81%)
  matrix products  37 us (7%)
  blocking collectives  24.9 us (5%)
  between operations  13.9 us (3%)
  other arithmetic  13.8 us (3%)
  local copies, waits for them, and re-layouts  6.95 us (1%)
    all_gather x1, waiting for transfers between devices, shards(): lax.all_gather(source_rows, 'seq', axis=0, tiled=True)  174 us
    all_gather x1, waiting for transfers between devices, shards(): lax.all_gather(low_weights[1], 'rep', axis=0, tiled=True)  90.2 us
    all_gather x1, waiting for transfers between devices, shards(): lax.all_gather(low_weights[0], 'rep', axis=0, tiled=True)  90.2 us
    all_gather x1, waiting for transfers between devices, shards(): lax.all_gather(low_weights[2], 'rep', axis=0, tiled=True)  76.4 us
    all_to_all x1, blocking collectives, shards(): lax.all_to_all(head_output, 'seq', split_axis=0, concat_axis=1, tiled=True)  24.9 us
    dot_general x1, matrix products, shards(): jnp.dot(lax.all_gather(source_rows, 'seq', axis=0, tiled=True), joined, p...  16.1 us
    dot_general x3, matrix products, one_block(): jnp.einsum('hqk,khd->qhd', probs, values3, preferred_element_type=jnp.flo...  11.4 us
  transfers between devices with their start and end apart: 4, of which 4 were waited for; matrix products, arithmetic and copies ran while one was open for 2% of the time, Pallas kernels for 0%

commit v1 on v0

v1 whole, which is shorter than its diff:
```python
import functools
import math

import jax
import jax.numpy as jnp
from jax import lax
from jax.experimental import pallas as pl
from jax.experimental.pallas import tpu as pltpu
from jax.sharding import PartitionSpec as P

HEAD = 128
STEPS = 50
EARLY = 64
SPACE = 15 * 1024 + 512

ZL = 4
NX = 4
NY = 4
NC = 2


def rep_perm(move):
    pairs = []
    for x in range(NX):
        for z in range(ZL):
            goal = move(x, z)
            if goal is not None:
                pairs.append((x * ZL + z, (goal[0] % NX) * ZL + goal[1]))
    return pairs


def seq_perm(move):
    pairs = []
    for h in range(2):
        for y in range(NY):
            for c in range(NC):
                a, b, d = move(h, y, c)
                pairs.append(((h * NY + y) * NC + c, (a * NY + b % NY) * NC + d))
    return pairs


X_UP = rep_perm(lambda x, z: (x + 1, z))
X_DOWN = rep_perm(lambda x, z: (x - 1, z))
Z_PAIR = rep_perm(lambda x, z: (x, z ^ 1))
Z_MIDDLE = rep_perm(lambda x, z: (x, 3 - z) if z in (1, 2) else None)
Z_OUTER = rep_perm(lambda x, z: (x, z ^ 1) if z in (1, 2) else None)
H_SWAP = seq_perm(lambda h, y, c: (1 - h, y, c))
Y_UP = seq_perm(lambda h, y, c: (h, y + 1, c))
Y_DOWN = seq_perm(lambda h, y, c: (h, y - 1, c))
C_SWAP = seq_perm(lambda h, y, c: (h, y, 1 - c))


def modulation(step_value, mod_base, mod_time, width):
    frac = 1.0 - step_value.astype(jnp.float32) / STEPS
    sigma = 5.0 * frac / (1.0 + 4.0 * frac)
    half_width = width // 2
    freqs = jnp.exp(-math.log(10000.0) * jnp.arange(half_width, dtype=jnp.float32) / half_width)
    angles = 1000.0 * sigma * freqs
    embedding = jnp.concatenate([jnp.cos(angles), jnp.sin(angles)])
    return (mod_base[0] + mod_time[0] * embedding, mod_base[1] + mod_time[1] * embedding)


def cast_kernel(q_ref, k_ref, v_ref, before_ref, out_ref):
    width = q_ref.shape[1]
    for n, ref in enumerate((q_ref, k_ref, v_ref)):
        low = ref[...].astype(jnp.bfloat16)
        out_ref[:, n * width : (n + 1) * width] = low


def cast_weights(w_query, w_key, w_value, before):
    rows, width = w_query.shape
    shape = jax.ShapeDtypeStruct((rows, 3 * width), jnp.bfloat16)
    return pl.pallas_call(
        cast_kernel,
        out_shape=shape,
        in_specs=[pl.BlockSpec(memory_space=pltpu.VMEM)] * 3 + [pl.BlockSpec(memory_space=pl.ANY)],
        name="cast_weights",
    )(w_query, w_key, w_value, before)


def modulate_kernel(rows_ref, shift_ref, scale_ref, all_ref, early_ref, late_ref):
    values = rows_ref[0].astype(jnp.float32)
    center = jnp.mean(values, axis=1, keepdims=True)
    moved = values - center
    spread = jnp.mean(moved * moved, axis=1, keepdims=True)
    normed = moved * lax.rsqrt(spread + 1e-06)
    result = (normed * (1.0 + scale_ref[...]) + shift_ref[...]).astype(jnp.bfloat16)
    early = early_ref.shape[0]
    all_ref[...] = result
    early_ref[...] = result[:early]
    late_ref[...] = result[early:]


def modulate(tokens, shift_row, scale_row, early):
    _, rows, width = tokens.shape
    return pl.pallas_call(
        modulate_kernel,
        out_shape=tuple(
            jax.ShapeDtypeStruct((count, width), jnp.bfloat16) for count in (rows, early, rows - early)
        ),
        name="modulate",
    )(tokens, shift_row[None], scale_row[None])


def gate_kernel(*refs):
    pass


class Order:
    def __init__(self, first):
        self.last = first
        self.flying = {}

    def gate(self, array, before=None):
        anywhere = pl.BlockSpec(memory_space=pl.ANY)
        others = [self.last] if before is None else [self.last, before]
        self.last = pl.pallas_call(
            gate_kernel,
            out_shape=jax.ShapeDtypeStruct(array.shape, array.dtype),
            in_specs=[anywhere] * (1 + len(others)),
            out_specs=anywhere,
            input_output_aliases={0: 0},
            scratch_shapes=[pltpu.VMEM((SPACE, 1024), jnp.float32)],
            compiler_params=pltpu.CompilerParams(vmem_limit_bytes=63 * 1024 * 1024),
            name="gate",
        )(array, *others)
        return self.last

    def start(self, name, array, axis, perm):
        self.flying[name] = lax.ppermute(array, axis, perm)

    def finish(self, name, before=None):
        return self.gate(self.flying.pop(name), before)


def load_weights(place_ref, first, weight_refs, w_ref, sem):
    depth = weight_refs[0].shape[0]
    copies = []
    for i, ref in enumerate(weight_refs):
        at = pl.multiple_of(place_ref[first + i] * depth, depth)
        copies.append(pltpu.make_async_copy(ref, w_ref.at[pl.ds(at, depth), :], sem.at[i]))
    return copies


def attend_kernel(count_ref, place_ref, near_ref, *refs, heads, pieces, n_tokens, n_weights):
    token_refs = refs[:n_tokens]
    weight_refs = refs[n_tokens : n_tokens + n_weights]
    out_ref, x_ref, w_ref, qkv_ref, k_ref, v_ref, near_sem, x_sem, w_sem = refs[n_tokens + n_weights :]
    half = near_ref.shape[0]
    tile = 256
    w_copies = load_weights(place_ref, 1 + len(pieces), weight_refs, w_ref, w_sem)
    near_copies = [
        pltpu.make_async_copy(near_ref.at[pl.ds(at, tile), :], x_ref.at[pl.ds(at, tile), :], near_sem.at[at // tile])
        for at in range(0, half, tile)
    ]
    x_copies = []
    for i, (source, first, rows) in enumerate(pieces):
        at = pl.multiple_of(half + place_ref[1 + i] * 16, 16)
        x_copies.append(
            pltpu.make_async_copy(
                token_refs[source].at[pl.ds(first, rows), :], x_ref.at[pl.ds(at, rows), :], x_sem.at[i]
            )
        )
    for copy in w_copies + near_copies[:1]:
        copy.start()
    for copy in w_copies:
        copy.wait()
    for copy in near_copies[1:] + x_copies:
        copy.start()
    for at in range(0, 2 * half, tile):
        if at < half:
            near_copies[at // tile].wait()
        elif at == half:
            for copy in x_copies:
                copy.wait()
        qkv_ref[at : at + tile, :] = jnp.dot(
            x_ref[at : at + tile, :], w_ref[...], preferred_element_type=jnp.float32
        ).astype(jnp.bfloat16)

    place = place_ref[0]
    width = heads * HEAD
    rows_at = lax.broadcasted_iota(jnp.int32, (half, HEAD), 0)
    for part in range(2):
        h_place = place if part == 0 else 1 - place
        valid = rows_at + h_place * half < count_ref[0]
        to = slice(part * half, (part + 1) * half)
        for head in range(heads):
            cols = slice(head * HEAD, (head + 1) * HEAD)
            keys_at = slice(width + head * HEAD, width + (head + 1) * HEAD)
            values_at = slice(2 * width + head * HEAD, 2 * width + (head + 1) * HEAD)
            first_key = jnp.where(
                place == 0,
                qkv_ref[0:1, keys_at].astype(jnp.float32),
                qkv_ref[half : half + 1, keys_at].astype(jnp.float32),
            )
            keys = qkv_ref[to, keys_at].astype(jnp.float32)
            k_ref[to, cols] = jnp.where(valid, keys, first_key).astype(jnp.bfloat16)
            values = qkv_ref[to, values_at].astype(jnp.float32)
            v_ref[head, to, :HEAD] = jnp.where(valid, values, 0.0).astype(jnp.bfloat16)
            v_ref[head, to, HEAD:] = jnp.where(valid, 1.0, 0.0).astype(jnp.bfloat16)

    factor = math.log2(math.e) / math.sqrt(HEAD)
    steps = half // tile

    @pl.loop(0, 2 * steps)
    def _(step):
        at = pl.ds(pl.multiple_of(step * tile, tile), tile)
        to = pl.ds(pl.multiple_of(((step + place * steps) % (2 * steps)) * tile, tile), tile)
        for head in range(heads):
            cols = slice(head * HEAD, (head + 1) * HEAD)
            scores = lax.dot_general(
                qkv_ref[at, cols], k_ref[:, cols], (((1,), (1,)), ((), ())), preferred_element_type=jnp.float32
            )
            top = jnp.max(scores, axis=1, keepdims=True)
            weights = jnp.exp2((scores - top) * factor).astype(jnp.bfloat16)
            result = jnp.dot(weights, v_ref[head], preferred_element_type=jnp.float32)
            out_ref[to, cols] = (result[:, :HEAD] / result[:, HEAD : HEAD + 1]).astype(jnp.bfloat16)


def attend_all(count, places, near, pieces, tokens, weight_blocks):
    half, width = near.shape
    columns = weight_blocks[0].shape[1]
    heads = columns // 3 // HEAD
    smem = pl.BlockSpec(memory_space=pltpu.SMEM)
    vmem = pl.BlockSpec(memory_space=pltpu.VMEM)
    anywhere = pl.BlockSpec(memory_space=pl.ANY)
    return pl.pallas_call(
        functools.partial(
            attend_kernel, heads=heads, pieces=pieces, n_tokens=len(tokens), n_weights=len(weight_blocks)
        ),
        out_shape=jax.ShapeDtypeStruct((2 * half, heads * HEAD), jnp.bfloat16),
        in_specs=[smem, smem] + [anywhere] * (1 + len(tokens) + len(weight_blocks)),
        out_specs=vmem,
        scratch_shapes=[
            pltpu.VMEM((2 * half, width), jnp.bfloat16),
            pltpu.VMEM((width, columns), jnp.bfloat16),
            pltpu.VMEM((2 * half, columns), jnp.bfloat16),
            pltpu.VMEM((2 * half, heads * HEAD), jnp.bfloat16),
            pltpu.VMEM((heads, 2 * half, 2 * HEAD), jnp.bfloat16),
            pltpu.SemaphoreType.DMA((half // 256,)),
            pltpu.SemaphoreType.DMA((len(pieces),)),
            pltpu.SemaphoreType.DMA((len(weight_blocks),)),
        ],
        compiler_params=pltpu.CompilerParams(vmem_limit_bytes=56 * 1024 * 1024),
        name="attend_all",
    )(count, places, near, *tokens, *weight_blocks)


def shards(tokens, steps, counts, mod_base, mod_time, w_query, w_key, w_value):
    width = tokens.shape[2]
    rep, seq = lax.axis_index("rep"), lax.axis_index("seq")
    x_at, z_at = rep // ZL, rep % ZL
    h_at, y_at, c_at = seq // (NY * NC), (seq // NC) % NY, seq % NC

    rows = tokens.shape[1]
    early, late = EARLY, rows - EARLY
    shift_row, scale_row = modulation(steps[0], mod_base, mod_time, width)
    mine, t0, t1 = modulate(tokens, shift_row, scale_row, early)
    groups = [[(h * NY + y) * NC + c for y in range(NY) for c in range(NC)] for h in range(2)]
    near = lax.all_gather(mine, "seq", axis=0, axis_index_groups=groups, tiled=True)
    own = cast_weights(w_query, w_key, w_value, mine)

    inner = (z_at == 1) | (z_at == 2)
    order = Order(own)
    order.start("z0", t0, "seq", H_SWAP)
    order.start("own_u", own, "rep", X_UP)
    order.start("own_d", own, "rep", X_DOWN)
    order.start("pair", own, "rep", Z_PAIR)
    order.start("mid0", own, "rep", Z_MIDDLE)
    own_u = order.finish("own_u")
    order.start("own_f", own_u, "rep", X_UP)
    own_d = order.finish("own_d")
    pair = order.finish("pair")
    order.start("mid1", pair, "rep", Z_MIDDLE)
    order.start("pair_u", pair, "rep", X_UP)
    order.start("pair_d", pair, "rep", X_DOWN)
    mid0 = order.finish("mid0")
    order.start("out0", mid0, "rep", Z_OUTER)
    z0 = order.finish("z0")
    away = lax.all_gather(z0, "seq", axis=0, axis_index_groups=groups, tiled=True)
    mid1 = order.finish("mid1")
    order.start("out1", mid1, "rep", Z_OUTER)
    own_f = order.finish("own_f")
    far0 = jnp.where(inner, mid0, order.finish("out0"))
    pair_u = order.finish("pair_u")
    order.start("far0_u", far0, "rep", X_UP)
    pair_d = order.finish("pair_d")
    order.start("far0_d", far0, "rep", X_DOWN)
    order.start("pair_f", pair_d, "rep", X_DOWN)
    far1 = jnp.where(inner, mid1, order.finish("out1", near))
    order.start("z1", order.gate(t1), "seq", H_SWAP)
    far0_u = order.finish("far0_u")
    order.start("far1_u", far1, "rep", X_UP)
    order.start("far0_f", far0_u, "rep", X_UP)
    far0_d = order.finish("far0_d")
    order.start("far1_d", far1, "rep", X_DOWN)
    pair_f = order.finish("pair_f")
    far1_u = order.finish("far1_u")
    far1_d = order.finish("far1_d")
    order.start("far1_f", far1_d, "rep", X_DOWN)
    far0_f = order.finish("far0_f")
    z1 = order.finish("z1")
    order.start("z1_u", z1, "seq", Y_UP)
    order.start("z1_d", z1, "seq", Y_DOWN)
    order.start("z1_c", z1, "seq", C_SWAP)
    z1_d = order.finish("z1_d")
    order.start("z1_f", z1_d, "seq", Y_DOWN)
    order.start("z1_dc", z1_d, "seq", C_SWAP)
    z1_u = order.finish("z1_u")
    order.start("z1_uc", z1_u, "seq", C_SWAP)
    far1_f = order.finish("far1_f")
    z1_f = order.finish("z1_f")
    order.start("z1_fc", z1_f, "seq", C_SWAP)
    z1_c, z1_dc, z1_uc, z1_fc = [order.flying.pop(name) for name in ("z1_c", "z1_dc", "z1_uc", "z1_fc")]

    slots = [z_at, z_at ^ 1, jnp.where(z_at < 2, 2, 1), jnp.where(z_at < 2, 3, 0)]
    weights, w_places = [], []
    for z_place, group in zip(slots, (
        (own, own_u, own_d, own_f), (pair, pair_u, pair_d, pair_f),
        (far0, far0_u, far0_d, far0_f), (far1, far1_u, far1_d, far1_f),
    )):
        for hop, block in zip((0, -1, 1, 2), group):
            weights.append(block)
            w_places.append(((x_at + hop) % NX) * ZL + z_place)
    w_places = jnp.stack(w_places).astype(jnp.int32)
    blocks = [away, z1, z1_c, z1_u, z1_uc, z1_d, z1_dc, z1_f, z1_fc]
    unit = rows // 16
    pieces, places = [], [h_at]
    for i in range(NY * NC):
        pieces.append((0, i * early, early))
        places.append(jnp.int32(i * unit))
    for hop in (0, -1, 1, 2):
        for other in range(2):
            pieces.append((len(pieces) - NY * NC + 1, 0, late))
            places.append((((y_at + hop) % NY) * NC + (c_at ^ other)) * unit + early // 16)
    places = jnp.concatenate([jnp.stack(places).astype(jnp.int32), w_places])
    head_output = attend_all(counts, places, near, pieces, blocks, weights)
    attended = lax.all_to_all(head_output, "seq", split_axis=0, concat_axis=1, tiled=True)
    return attended[None]


def solution(mesh):
    in_specs = (
        P("rep", "seq", None),
        P("rep"),
        P("rep"),
        P(),
        P(),
        P("rep", "seq"),
        P("rep", "seq"),
        P("rep", "seq"),
    )
    out_specs = P("rep", "seq", None)
    return jax.shard_map(shards, mesh=mesh, in_specs=in_specs, out_specs=out_specs, check_vma=False)
```

time: 530 us -> 212 us (0.40)
  the two profiles are of different devices: /device:TPU:2 before, /device:TPU:33 now
where the time goes in v1:
time: 212 us
  waiting for transfers between devices  70.9 us (33%)
  starting transfers between devices  44.6 us (21%)
  Pallas kernels  37.1 us (18%)
  blocking collectives  29.4 us (14%)
  between operations  14.9 us (7%)
  local copies, waits for them, and re-layouts  9.05 us (4%)
  other arithmetic  5.66 us (3%)
    ppermute x26, waiting for transfers between devices, start(): self.flying[name] = lax.ppermute(array, axis, perm)  70.9 us
    ppermute x26, starting transfers between devices, start(): self.flying[name] = lax.ppermute(array, axis, perm)  44.5 us
    pallas_call x1, Pallas kernels, attend_all(): pl.pallas_call(functools.partial(attend_kernel, heads=heads, pieces=piece...  31.8 us
    all_to_all x1, blocking collectives, shards(): lax.all_to_all(head_output, 'seq', split_axis=0, concat_axis=1, tiled=True)  29.4 us
    unnamed x20, local copies, waits for them, and re-layouts  6.78 us
  transfers between devices with their start and end apart: 28, of which 13 were waited for; matrix products, arithmetic and copies ran while one was open for 2% of the time, Pallas kernels for 1%

profile of v1, /device:TPU:33, one launch (start us, length us, event | category | flops | bytes accessed | tf_op | source)
XLA Modules:
  0.0 211.7 jit_solution(11682367714476045991)
XLA Ops:
  7.6 1.6 multiply_add_fusion
  9.1 3.3 %modulate.1 = (bf16[96,5120]{1,0:T(8,128)(2,1)}, bf16[64,5120]{1,0:T(8,128)(2,1)}, bf16[32,5120]{1,0:T(8,128)(2,1)}) custom-call(bf16[1,96,5120]{2,1,0:T(8,128)(2,1)} %rows_ref.1, f32[1,5120]{1,0:T(1,128)} %get-tuple-element.12.shift_ref, f32[1,5120]{1,0:T(1,128)} %get-tuple-element.11.scale_ref), custom_call_target="tpu_custom_call" | custom-call | tf_op jit(solution)/shard_map/modulate/pallas_call | solution.py:96
  12.5 6.1 %collective-permute-start = (bf16[64,5120]{1,0:T(8,128)(2,1)}, bf16[64,5120]{1,0:T(8,128)(2,1)S(1)}, u32[]{:S(2)}, u32[]{:S(2)}) collective-permute-start(bf16[64,5120]{1,0:T(8,128)(2,1)} %get-tuple-element.9), channel_id=1, source_target_pairs={{0,8},{1,9},{2,10},{3,11},{4,12},{5,13},{6,14},{7,15},{8,0},{9,1},... | collective-permute-start | bytes 1966088 | tf_op jit(solution)/shard_map/ppermute | solution.py:130
  18.6 2.0 cast_weights.1.refs_1_.refs_9_
  21.8 1.5 collective-permute-start.3
  24.0 2.6 %collective-permute-start.1 = (bf16[320,768]{1,0:T(8,128)(2,1)}, bf16[320,768]{1,0:T(8,128)(2,1)}, u32[]{:S(2)}, u32[]{:S(2)}) collective-permute-start(bf16[320,768]{1,0:T(8,128)(2,1)} %cast_weights.1.refs_1_.refs_9_), channel_id=1, source_target_pairs={{16,32},{32,16},{80,96},{96,80},{144,160},{160,144},{208,224},{224... | collective-permute-start | bytes 1474568 | tf_op jit(solution)/shard_map/ppermute | solution.py:130
  26.7 7.2 %collective-permute-done.4.refs_0_ = bf16[320,768]{1,0:T(8,128)(2,1)} collective-permute-done((bf16[320,768]{1,0:T(8,128)(2,1)}, bf16[320,768]{1,0:T(8,128)(2,1)}, u32[]{:S(2)}, u32[]{:S(2)}) %collective-permute-start.4) | collective-permute-done | bytes 491552 | tf_op jit(solution)/shard_map/ppermute | solution.py:130
  33.9 23.9 %collective-permute-done.2.refs_0_ = bf16[320,768]{1,0:T(8,128)(2,1)} collective-permute-done((bf16[320,768]{1,0:T(8,128)(2,1)}, bf16[320,768]{1,0:T(8,128)(2,1)}, u32[]{:S(2)}, u32[]{:S(2)}) %collective-permute-start.2) | collective-permute-done | bytes 491552 | tf_op jit(solution)/shard_map/ppermute | solution.py:130
  59.7 3.1 %collective-permute-start.5 = (bf16[320,768]{1,0:T(8,128)(2,1)}, bf16[320,768]{1,0:T(8,128)(2,1)}, u32[]{:S(2)}, u32[]{:S(2)}) collective-permute-start(bf16[320,768]{1,0:T(8,128)(2,1)} %gate.25.refs_1_.refs_13_), channel_id=1, source_target_pairs={{16,32},{32,16},{80,96},{96,80},{144,160},{160,144},{208,224},{224... | collective-permute-start | bytes 1474568 | tf_op jit(solution)/shard_map/ppermute | solution.py:130
  62.7 1.3 collective-permute-start.10
  64.0 1.3 collective-permute-start.9
  66.7 1.5 collective-permute-start.7
  68.1 6.0 %collective-permute-done.5.refs_0_ = bf16[320,768]{1,0:T(8,128)(2,1)} collective-permute-done((bf16[320,768]{1,0:T(8,128)(2,1)}, bf16[320,768]{1,0:T(8,128)(2,1)}, u32[]{:S(2)}, u32[]{:S(2)}) %collective-permute-start.5) | collective-permute-done | bytes 491552 | tf_op jit(solution)/shard_map/ppermute | solution.py:130
  74.1 2.1 collective-permute-start.6
  77.8 1.9 broadcast_select_fusion.1.refs_17_
  80.8 1.6 collective-permute-start.17
  82.4 4.5 %collective-permute-done.8.refs_0_ = bf16[320,768]{1,0:T(8,128)(2,1)} collective-permute-done((bf16[320,768]{1,0:T(8,128)(2,1)}, bf16[320,768]{1,0:T(8,128)(2,1)}, u32[]{:S(2)}, u32[]{:S(2)}) %collective-permute-start.8) | collective-permute-done | bytes 491552 | tf_op jit(solution)/shard_map/ppermute | solution.py:130
  88.1 1.9 broadcast_select_fusion.refs_21_
  90.2 2.5 %collective-permute-start.14 = (bf16[320,768]{1,0:T(8,128)(2,1)}, bf16[320,768]{1,0:T(8,128)(2,1)}, u32[]{:S(2)}, u32[]{:S(2)}) collective-permute-start(bf16[320,768]{1,0:T(8,128)(2,1)} %broadcast_select_fusion.refs_21_), channel_id=1, source_target_pairs={{0,192},{16,208},{32,224},{48,240},{64,0},{80,16},{96,32},{112,48}... | collective-permute-start | bytes 1474568 | tf_op jit(solution)/shard_map/ppermute | solution.py:130
  92.7 4.7 %collective-permute-done.12.refs_0_ = bf16[320,768]{1,0:T(8,128)(2,1)S(1)} collective-permute-done((bf16[320,768]{1,0:T(8,128)(2,1)}, bf16[320,768]{1,0:T(8,128)(2,1)S(1)}, u32[]{:S(2)}, u32[]{:S(2)}) %collective-permute-start.12) | collective-permute-done | bytes 491552 | tf_op jit(solution)/shard_map/ppermute | solution.py:130
  99.2 3.0 %collective-permute-done.16.refs_0_ = bf16[320,768]{1,0:T(8,128)(2,1)} collective-permute-done((bf16[320,768]{1,0:T(8,128)(2,1)}, bf16[320,768]{1,0:T(8,128)(2,1)}, u32[]{:S(2)}, u32[]{:S(2)}) %collective-permute-start.16) | collective-permute-done | bytes 491552 | tf_op jit(solution)/shard_map/ppermute | solution.py:130
  102.2 5.7 %collective-permute-done.15.refs_0_ = bf16[320,768]{1,0:T(8,128)(2,1)} collective-permute-done((bf16[320,768]{1,0:T(8,128)(2,1)}, bf16[320,768]{1,0:T(8,128)(2,1)}, u32[]{:S(2)}, u32[]{:S(2)}) %collective-permute-start.15) | collective-permute-done | bytes 491552 | tf_op jit(solution)/shard_map/ppermute | solution.py:130
  107.9 4.8 %collective-permute-done.14.refs_0_ = bf16[320,768]{1,0:T(8,128)(2,1)} collective-permute-done((bf16[320,768]{1,0:T(8,128)(2,1)}, bf16[320,768]{1,0:T(8,128)(2,1)}, u32[]{:S(2)}, u32[]{:S(2)}) %collective-permute-start.14) | collective-permute-done | bytes 491552 | tf_op jit(solution)/shard_map/ppermute | solution.py:130
  112.8 5.6 %collective-permute-done.13.refs_0_ = bf16[320,768]{1,0:T(8,128)(2,1)S(1)} collective-permute-done((bf16[320,768]{1,0:T(8,128)(2,1)}, bf16[320,768]{1,0:T(8,128)(2,1)S(1)}, u32[]{:S(2)}, u32[]{:S(2)}) %collective-permute-start.13) | collective-permute-done | bytes 491552 | tf_op jit(solution)/shard_map/ppermute | solution.py:130
  119.1 2.7 %collective-permute-start.20 = (bf16[32,5120]{1,0:T(8,128)(2,1)}, bf16[32,5120]{1,0:T(8,128)(2,1)}, u32[]{:S(2)}, u32[]{:S(2)}) collective-permute-start(bf16[32,5120]{1,0:T(8,128)(2,1)} %gate.41.refs_1_), channel_id=1, source_target_pairs={{0,6},{1,7},{2,0},{3,1},{4,2},{5,3},{6,4},{7,5},{8,14},{9,15},{10,... | collective-permute-start | bytes 983048 | tf_op jit(solution)/shard_map/ppermute | solution.py:130
  121.9 1.4 collective-permute-start.24
  123.2 4.3 %collective-permute-done.20.refs_0_ = bf16[32,5120]{1,0:T(8,128)(2,1)} collective-permute-done((bf16[32,5120]{1,0:T(8,128)(2,1)}, bf16[32,5120]{1,0:T(8,128)(2,1)}, u32[]{:S(2)}, u32[]{:S(2)}) %collective-permute-start.20) | collective-permute-done | bytes 327712 | tf_op jit(solution)/shard_map/ppermute | solution.py:130
  127.5 3.4 %collective-permute-start.23 = (bf16[32,5120]{1,0:T(8,128)(2,1)}, bf16[32,5120]{1,0:T(8,128)(2,1)}, u32[]{:S(2)}, u32[]{:S(2)}) collective-permute-start(bf16[32,5120]{1,0:T(8,128)(2,1)} %gate.42.refs_1_.refs_5_), channel_id=1, source_target_pairs={{0,6},{1,7},{2,0},{3,1},{4,2},{5,3},{6,4},{7,5},{8,14},{9,15},{10,... | collective-permute-start | bytes 983048 | tf_op jit(solution)/shard_map/ppermute | solution.py:130
  130.9 2.9 %collective-permute-start.18 = (bf16[32,5120]{1,0:T(8,128)(2,1)}, bf16[32,5120]{1,0:T(8,128)(2,1)}, u32[]{:S(2)}, u32[]{:S(2)}) collective-permute-start(bf16[32,5120]{1,0:T(8,128)(2,1)} %gate.41.refs_1_), channel_id=1, source_target_pairs={{0,1},{1,0},{2,3},{3,2},{4,5},{5,4},{6,7},{7,6},{8,9},{9,8},{10,11... | collective-permute-start | bytes 983048 | tf_op jit(solution)/shard_map/ppermute | solution.py:130
  136.3 2.9 %collective-permute-start.25 = (bf16[32,5120]{1,0:T(8,128)(2,1)}, bf16[32,5120]{1,0:T(8,128)(2,1)S(1)}, u32[]{:S(2)}, u32[]{:S(2)}) collective-permute-start(bf16[32,5120]{1,0:T(8,128)(2,1)} %gate.45.refs_7_), channel_id=1, source_target_pairs={{0,1},{1,0},{2,3},{3,2},{4,5},{5,4},{6,7},{7,6},{8,9},{9,8},{10,11... | collective-permute-start | bytes 983048 | tf_op jit(solution)/shard_map/ppermute | solution.py:130
  141.9 31.8 %attend_all.1 = bf16[1536,256]{1,0:T(8,128)(2,1)} custom-call(s32[1]{0:T(128)S(6)} %copy.57.count_ref, s32[33]{0:T(128)} %concatenate.8.place_ref, bf16[768,5120]{1,0:T(8,128)(2,1)} %all-gather.3.cloned.1.call-done.refs_2_.near_ref, bf16[512,5120]{1,0:T(8,128)(2,1)} %all-gather.5.cloned.1.call-done.refs_0_, bf16[32,5120]{1,0:T(8,128)(2,1)} %gate.41.refs_1_, ...), custom_call_target="tpu_custom_call" | custom-call | tf_op jit(solution)/shard_map/attend_all/pallas_call | solution.py:227
  173.7 29.4 %all_to_all.16 = bf16[16,96,256]{2,1,0:T(8,128)(2,1)S(1)} all-to-all(bf16[16,96,256]{2,1,0:T(8,128)(2,1)} %bitcast.28), channel_id=1, replica_groups=mesh['rep'=16,'seq'=16] {'seq'}, dimensions={0} | all-to-all | bytes 1572864 | tf_op jit(solution)/shard_map/all_to_all | solution.py:338
  (80 shorter events, 18.5 us)
Async XLA Ops:
  6.5 81.6 %all-gather.3.cloned.1.call-start = ((), (), s32[]{:S(2)}) async-start(), calls=%async_computation.1 | async-start | bytes 8847360 | tf_op jit(solution)/shard_map/all_gather | solution.py:260
  12.5 128.0 %all-gather.5.cloned.1.call-start = ((), (), s32[]{:S(2)}) async-start(), calls=%async_computation.2 | async-start | bytes 5898240 | tf_op jit(solution)/shard_map/all_gather | solution.py:280
  12.5 46.3 %collective-permute-start = (bf16[64,5120]{1,0:T(8,128)(2,1)}, bf16[64,5120]{1,0:T(8,128)(2,1)S(1)}, u32[]{:S(2)}, u32[]{:S(2)}) collective-permute-start(bf16[64,5120]{1,0:T(8,128)(2,1)} %get-tuple-element.9), channel_id=1, source_target_pairs={{0,8},{1,9},{2,10},{3,11},{4,12},{5,13},{6,14},{7,15},{8,0},{9,1},... | collective-permute-start | bytes 1966088 | tf_op jit(solution)/shard_map/ppermute | solution.py:130
  20.6 13.3 %collective-permute-start.4 = (bf16[320,768]{1,0:T(8,128)(2,1)}, bf16[320,768]{1,0:T(8,128)(2,1)}, u32[]{:S(2)}, u32[]{:S(2)}) collective-permute-start(bf16[320,768]{1,0:T(8,128)(2,1)} %cast_weights.1.refs_1_.refs_9_), channel_id=1, source_target_pairs={{0,64},{16,80},{32,96},{48,112},{64,128},{80,144},{96,160},{112,17... | collective-permute-start | bytes 1474568 | tf_op jit(solution)/shard_map/ppermute | solution.py:130
  21.8 12.1 %collective-permute-start.3 = (bf16[320,768]{1,0:T(8,128)(2,1)}, bf16[320,768]{1,0:T(8,128)(2,1)}, u32[]{:S(2)}, u32[]{:S(2)}) collective-permute-start(bf16[320,768]{1,0:T(8,128)(2,1)} %cast_weights.1.refs_1_.refs_9_), channel_id=1, source_target_pairs={{0,192},{16,208},{32,224},{48,240},{64,0},{80,16},{96,32},{112,48}... | collective-permute-start | bytes 1474568 | tf_op jit(solution)/shard_map/ppermute | solution.py:130
  23.3 34.5 %collective-permute-start.2 = (bf16[320,768]{1,0:T(8,128)(2,1)}, bf16[320,768]{1,0:T(8,128)(2,1)}, u32[]{:S(2)}, u32[]{:S(2)}) collective-permute-start(bf16[320,768]{1,0:T(8,128)(2,1)} %cast_weights.1.refs_1_.refs_9_), channel_id=1, source_target_pairs={{0,16},{16,0},{32,48},{48,32},{64,80},{80,64},{96,112},{112,96},{1... | collective-permute-start | bytes 1474568 | tf_op jit(solution)/shard_map/ppermute | solution.py:130
  24.0 34.8 %collective-permute-start.1 = (bf16[320,768]{1,0:T(8,128)(2,1)}, bf16[320,768]{1,0:T(8,128)(2,1)}, u32[]{:S(2)}, u32[]{:S(2)}) collective-permute-start(bf16[320,768]{1,0:T(8,128)(2,1)} %cast_weights.1.refs_1_.refs_9_), channel_id=1, source_target_pairs={{16,32},{32,16},{80,96},{96,80},{144,160},{160,144},{208,224},{224... | collective-permute-start | bytes 1474568 | tf_op jit(solution)/shard_map/ppermute | solution.py:130
  58.8 0.8 copy-start
  59.7 14.4 %collective-permute-start.5 = (bf16[320,768]{1,0:T(8,128)(2,1)}, bf16[320,768]{1,0:T(8,128)(2,1)}, u32[]{:S(2)}, u32[]{:S(2)}) collective-permute-start(bf16[320,768]{1,0:T(8,128)(2,1)} %gate.25.refs_1_.refs_13_), channel_id=1, source_target_pairs={{16,32},{32,16},{80,96},{96,80},{144,160},{160,144},{208,224},{224... | collective-permute-start | bytes 1474568 | tf_op jit(solution)/shard_map/ppermute | solution.py:130
  62.7 13.5 %collective-permute-start.10 = (bf16[320,768]{1,0:T(8,128)(2,1)}, bf16[320,768]{1,0:T(8,128)(2,1)S(1)}, u32[]{:S(2)}, u32[]{:S(2)}) collective-permute-start(bf16[320,768]{1,0:T(8,128)(2,1)} %gate.23.refs_1_.refs_10_), channel_id=1, source_target_pairs={{0,64},{16,80},{32,96},{48,112},{64,128},{80,144},{96,160},{112,17... | collective-permute-start | bytes 1474568 | tf_op jit(solution)/shard_map/ppermute | solution.py:130
  64.0 13.0 %collective-permute-start.9 = (bf16[320,768]{1,0:T(8,128)(2,1)}, bf16[320,768]{1,0:T(8,128)(2,1)S(1)}, u32[]{:S(2)}, u32[]{:S(2)}) collective-permute-start(bf16[320,768]{1,0:T(8,128)(2,1)} %gate.26.refs_1_), channel_id=1, source_target_pairs={{16,0},{32,48},{80,64},{96,112},{144,128},{160,176},{208,192},{224... | collective-permute-start | bytes 1474568 | tf_op jit(solution)/shard_map/ppermute | solution.py:130
  65.4 21.5 %collective-permute-start.8 = (bf16[320,768]{1,0:T(8,128)(2,1)}, bf16[320,768]{1,0:T(8,128)(2,1)}, u32[]{:S(2)}, u32[]{:S(2)}) collective-permute-start(bf16[320,768]{1,0:T(8,128)(2,1)} %gate.25.refs_1_.refs_13_), channel_id=1, source_target_pairs={{0,64},{16,80},{32,96},{48,112},{64,128},{80,144},{96,160},{112,17... | collective-permute-start | bytes 1474568 | tf_op jit(solution)/shard_map/ppermute | solution.py:130
  66.7 20.2 %collective-permute-start.7 = (bf16[320,768]{1,0:T(8,128)(2,1)}, bf16[320,768]{1,0:T(8,128)(2,1)}, u32[]{:S(2)}, u32[]{:S(2)}) collective-permute-start(bf16[320,768]{1,0:T(8,128)(2,1)} %gate.25.refs_1_.refs_13_), channel_id=1, source_target_pairs={{0,192},{16,208},{32,224},{48,240},{64,0},{80,16},{96,32},{112,48}... | collective-permute-start | bytes 1474568 | tf_op jit(solution)/shard_map/ppermute | solution.py:130
  74.1 14.1 %collective-permute-start.6 = (bf16[320,768]{1,0:T(8,128)(2,1)}, bf16[320,768]{1,0:T(8,128)(2,1)}, u32[]{:S(2)}, u32[]{:S(2)}) collective-permute-start(bf16[320,768]{1,0:T(8,128)(2,1)} %gate.28.refs_1_), channel_id=1, source_target_pairs={{16,0},{32,48},{80,64},{96,112},{144,128},{160,176},{208,192},{224... | collective-permute-start | bytes 1474568 | tf_op jit(solution)/shard_map/ppermute | solution.py:130
  77.0 0.8 copy-start.6
  79.7 17.7 %collective-permute-start.12 = (bf16[320,768]{1,0:T(8,128)(2,1)}, bf16[320,768]{1,0:T(8,128)(2,1)S(1)}, u32[]{:S(2)}, u32[]{:S(2)}) collective-permute-start(bf16[320,768]{1,0:T(8,128)(2,1)} %broadcast_select_fusion.1.refs_17_), channel_id=1, source_target_pairs={{0,64},{16,80},{32,96},{48,112},{64,128},{80,144},{96,160},{112,17... | collective-permute-start | bytes 1474568 | tf_op jit(solution)/shard_map/ppermute | solution.py:130
  80.8 17.4 %collective-permute-start.17 = (bf16[320,768]{1,0:T(8,128)(2,1)}, bf16[320,768]{1,0:T(8,128)(2,1)S(1)}, u32[]{:S(2)}, u32[]{:S(2)}) collective-permute-start(bf16[320,768]{1,0:T(8,128)(2,1)} %broadcast_select_fusion.1.refs_17_), channel_id=1, source_target_pairs={{0,192},{16,208},{32,224},{48,240},{64,0},{80,16},{96,32},{112,48}... | collective-permute-start | bytes 1474568 | tf_op jit(solution)/shard_map/ppermute | solution.py:130
  86.9 15.4 %collective-permute-start.16 = (bf16[320,768]{1,0:T(8,128)(2,1)}, bf16[320,768]{1,0:T(8,128)(2,1)}, u32[]{:S(2)}, u32[]{:S(2)}) collective-permute-start(bf16[320,768]{1,0:T(8,128)(2,1)} %gate.32.refs_1_.refs_15_), channel_id=1, source_target_pairs={{0,192},{16,208},{32,224},{48,240},{64,0},{80,16},{96,32},{112,48}... | collective-permute-start | bytes 1474568 | tf_op jit(solution)/shard_map/ppermute | solution.py:130
  90.0 17.9 %collective-permute-start.15 = (bf16[320,768]{1,0:T(8,128)(2,1)}, bf16[320,768]{1,0:T(8,128)(2,1)}, u32[]{:S(2)}, u32[]{:S(2)}) collective-permute-start(bf16[320,768]{1,0:T(8,128)(2,1)} %broadcast_select_fusion.refs_21_), channel_id=1, source_target_pairs={{0,64},{16,80},{32,96},{48,112},{64,128},{80,144},{96,160},{112,17... | collective-permute-start | bytes 1474568 | tf_op jit(solution)/shard_map/ppermute | solution.py:130
  90.2 22.5 %collective-permute-start.14 = (bf16[320,768]{1,0:T(8,128)(2,1)}, bf16[320,768]{1,0:T(8,128)(2,1)}, u32[]{:S(2)}, u32[]{:S(2)}) collective-permute-start(bf16[320,768]{1,0:T(8,128)(2,1)} %broadcast_select_fusion.refs_21_), channel_id=1, source_target_pairs={{0,192},{16,208},{32,224},{48,240},{64,0},{80,16},{96,32},{112,48}... | collective-permute-start | bytes 1474568 | tf_op jit(solution)/shard_map/ppermute | solution.py:130
  97.4 0.8 copy-start.3
  98.2 20.2 %collective-permute-start.13 = (bf16[320,768]{1,0:T(8,128)(2,1)}, bf16[320,768]{1,0:T(8,128)(2,1)S(1)}, u32[]{:S(2)}, u32[]{:S(2)}) collective-permute-start(bf16[320,768]{1,0:T(8,128)(2,1)} %gate.35.refs_1_.refs_18_), channel_id=1, source_target_pairs={{0,64},{16,80},{32,96},{48,112},{64,128},{80,144},{96,160},{112,17... | collective-permute-start | bytes 1474568 | tf_op jit(solution)/shard_map/ppermute | solution.py:130
  98.2 1.0 copy-start.1
  98.2 20.9 %collective-permute-start.11 = (bf16[32,5120]{1,0:T(8,128)(2,1)}, bf16[32,5120]{1,0:T(8,128)(2,1)}, u32[]{:S(2)}, u32[]{:S(2)}) collective-permute-start(bf16[32,5120]{1,0:T(8,128)(2,1)} %gate.34.refs_1_), channel_id=1, source_target_pairs={{0,8},{1,9},{2,10},{3,11},{4,12},{5,13},{6,14},{7,15},{8,0},{9,1},... | collective-permute-start | bytes 983048 | tf_op jit(solution)/shard_map/ppermute | solution.py:130
  119.1 8.4 %collective-permute-start.20 = (bf16[32,5120]{1,0:T(8,128)(2,1)}, bf16[32,5120]{1,0:T(8,128)(2,1)}, u32[]{:S(2)}, u32[]{:S(2)}) collective-permute-start(bf16[32,5120]{1,0:T(8,128)(2,1)} %gate.41.refs_1_), channel_id=1, source_target_pairs={{0,6},{1,7},{2,0},{3,1},{4,2},{5,3},{6,4},{7,5},{8,14},{9,15},{10,... | collective-permute-start | bytes 983048 | tf_op jit(solution)/shard_map/ppermute | solution.py:130
  121.9 13.7 %collective-permute-start.24 = (bf16[320,768]{1,0:T(8,128)(2,1)}, bf16[320,768]{1,0:T(8,128)(2,1)S(1)}, u32[]{:S(2)}, u32[]{:S(2)}) collective-permute-start(bf16[320,768]{1,0:T(8,128)(2,1)} %gate.39.refs_1_.refs_23_), channel_id=1, source_target_pairs={{0,192},{16,208},{32,224},{48,240},{64,0},{80,16},{96,32},{112,48}... | collective-permute-start | bytes 1474568 | tf_op jit(solution)/shard_map/ppermute | solution.py:130
  123.2 10.6 %collective-permute-start.19 = (bf16[32,5120]{1,0:T(8,128)(2,1)}, bf16[32,5120]{1,0:T(8,128)(2,1)S(1)}, u32[]{:S(2)}, u32[]{:S(2)}) collective-permute-start(bf16[32,5120]{1,0:T(8,128)(2,1)} %gate.41.refs_1_), channel_id=1, source_target_pairs={{0,2},{1,3},{2,4},{3,5},{4,6},{5,7},{6,0},{7,1},{8,10},{9,11},{10,... | collective-permute-start | bytes 983048 | tf_op jit(solution)/shard_map/ppermute | solution.py:130
  127.5 8.8 %collective-permute-start.23 = (bf16[32,5120]{1,0:T(8,128)(2,1)}, bf16[32,5120]{1,0:T(8,128)(2,1)}, u32[]{:S(2)}, u32[]{:S(2)}) collective-permute-start(bf16[32,5120]{1,0:T(8,128)(2,1)} %gate.42.refs_1_.refs_5_), channel_id=1, source_target_pairs={{0,6},{1,7},{2,0},{3,1},{4,2},{5,3},{6,4},{7,5},{8,14},{9,15},{10,... | collective-permute-start | bytes 983048 | tf_op jit(solution)/shard_map/ppermute | solution.py:130
  130.9 9.5 %collective-permute-start.18 = (bf16[32,5120]{1,0:T(8,128)(2,1)}, bf16[32,5120]{1,0:T(8,128)(2,1)}, u32[]{:S(2)}, u32[]{:S(2)}) collective-permute-start(bf16[32,5120]{1,0:T(8,128)(2,1)} %gate.41.refs_1_), channel_id=1, source_target_pairs={{0,1},{1,0},{2,3},{3,2},{4,5},{5,4},{6,7},{7,6},{8,9},{9,8},{10,11... | collective-permute-start | bytes 983048 | tf_op jit(solution)/shard_map/ppermute | solution.py:130
  133.8 6.6 %collective-permute-start.22 = (bf16[32,5120]{1,0:T(8,128)(2,1)}, bf16[32,5120]{1,0:T(8,128)(2,1)}, u32[]{:S(2)}, u32[]{:S(2)}) collective-permute-start(bf16[32,5120]{1,0:T(8,128)(2,1)} %gate.42.refs_1_.refs_5_), channel_id=1, source_target_pairs={{0,1},{1,0},{2,3},{3,2},{4,5},{5,4},{6,7},{7,6},{8,9},{9,8},{10,11... | collective-permute-start | bytes 983048 | tf_op jit(solution)/shard_map/ppermute | solution.py:130
  134.5 5.9 %collective-permute-start.21 = (bf16[32,5120]{1,0:T(8,128)(2,1)}, bf16[32,5120]{1,0:T(8,128)(2,1)S(1)}, u32[]{:S(2)}, u32[]{:S(2)}) collective-permute-start(bf16[32,5120]{1,0:T(8,128)(2,1)} %gate.43.refs_1_.refs_3_), channel_id=1, source_target_pairs={{0,1},{1,0},{2,3},{3,2},{4,5},{5,4},{6,7},{7,6},{8,9},{9,8},{10,11... | collective-permute-start | bytes 983048 | tf_op jit(solution)/shard_map/ppermute | solution.py:130
  136.3 4.3 %collective-permute-start.25 = (bf16[32,5120]{1,0:T(8,128)(2,1)}, bf16[32,5120]{1,0:T(8,128)(2,1)S(1)}, u32[]{:S(2)}, u32[]{:S(2)}) collective-permute-start(bf16[32,5120]{1,0:T(8,128)(2,1)} %gate.45.refs_7_), channel_id=1, source_target_pairs={{0,1},{1,0},{2,3},{3,2},{4,5},{5,4},{6,7},{7,6},{8,9},{9,8},{10,11... | collective-permute-start | bytes 983048 | tf_op jit(solution)/shard_map/ppermute | solution.py:130
  (6 other events, 4.6 us)
Sparse Core Ops, SparseCore 0:
  12.6 53.1 all-gather.2
  67.6 39.2 all-gather.4

commit v2 on v1

--- a/solution.py
+++ b/solution.py
@@ -270,6 +270,7 @@
     own_u = order.finish("own_u")
     order.start("own_f", own_u, "rep", X_UP)
     own_d = order.finish("own_d")
+    own_f = order.finish("own_f")
     pair = order.finish("pair")
     order.start("mid1", pair, "rep", Z_MIDDLE)
     order.start("pair_u", pair, "rep", X_UP)
@@ -280,29 +281,29 @@
     away = lax.all_gather(z0, "seq", axis=0, axis_index_groups=groups, tiled=True)
     mid1 = order.finish("mid1")
     order.start("out1", mid1, "rep", Z_OUTER)
-    own_f = order.finish("own_f")
+    pair_u = order.finish("pair_u")
+    order.start("pair_f", pair_u, "rep", X_UP)
     far0 = jnp.where(inner, mid0, order.finish("out0"))
-    pair_u = order.finish("pair_u")
     order.start("far0_u", far0, "rep", X_UP)
     pair_d = order.finish("pair_d")
     order.start("far0_d", far0, "rep", X_DOWN)
-    order.start("pair_f", pair_d, "rep", X_DOWN)
     far1 = jnp.where(inner, mid1, order.finish("out1", near))
     order.start("z1", order.gate(t1), "seq", H_SWAP)
-    far0_u = order.finish("far0_u")
-    order.start("far1_u", far1, "rep", X_UP)
-    order.start("far0_f", far0_u, "rep", X_UP)
-    far0_d = order.finish("far0_d")
     order.start("far1_d", far1, "rep", X_DOWN)
     pair_f = order.finish("pair_f")
-    far1_u = order.finish("far1_u")
-    far1_d = order.finish("far1_d")
-    order.start("far1_f", far1_d, "rep", X_DOWN)
-    far0_f = order.finish("far0_f")
+    order.start("far1_u", far1, "rep", X_UP)
+    far0_u = order.finish("far0_u")
+    far0_d = order.finish("far0_d")
+    order.start("far0_f", far0_d, "rep", X_DOWN)
     z1 = order.finish("z1")
     order.start("z1_u", z1, "seq", Y_UP)
     order.start("z1_d", z1, "seq", Y_DOWN)
+    far1_u = order.finish("far1_u")
+    order.start("far1_f", far1_u, "rep", X_UP)
+    far1_d = order.finish("far1_d")
     order.start("z1_c", z1, "seq", C_SWAP)
+    far0_f = order.finish("far0_f")
+    z1_c = order.finish("z1_c")
     z1_d = order.finish("z1_d")
     order.start("z1_f", z1_d, "seq", Y_DOWN)
     order.start("z1_dc", z1_d, "seq", C_SWAP)
@@ -311,7 +312,7 @@
     far1_f = order.finish("far1_f")
     z1_f = order.finish("z1_f")
     order.start("z1_fc", z1_f, "seq", C_SWAP)
-    z1_c, z1_dc, z1_uc, z1_fc = [order.flying.pop(name) for name in ("z1_c", "z1_dc", "z1_uc", "z1_fc")]
+    z1_dc, z1_uc, z1_fc = [order.flying.pop(name) for name in ("z1_dc", "z1_uc", "z1_fc")]
 
     slots = [z_at, z_at ^ 1, jnp.where(z_at < 2, 2, 1), jnp.where(z_at < 2, 3, 0)]
     weights, w_places = [], []

time: 212 us -> 206 us (0.972)
  the two profiles are of different devices: /device:TPU:33 before, /device:TPU:2 now
where the time goes in v2:
time: 206 us
  waiting for transfers between devices  72.6 us (35%)
  starting transfers between devices  38.6 us (19%)
  Pallas kernels  37.2 us (18%)
  blocking collectives  29.4 us (14%)
  between operations  14.9 us (7%)
  local copies, waits for them, and re-layouts  7.79 us (4%)
  other arithmetic  5.65 us (3%)
    ppermute x26, waiting for transfers between devices, start(): self.flying[name] = lax.ppermute(array, axis, perm)  72.5 us
    ppermute x26, starting transfers between devices, start(): self.flying[name] = lax.ppermute(array, axis, perm)  38.6 us
    pallas_call x1, Pallas kernels, attend_all(): pl.pallas_call(functools.partial(attend_kernel, heads=heads, pieces=piece...  31.8 us
    all_to_all x1, blocking collectives, shards(): lax.all_to_all(head_output, 'seq', split_axis=0, concat_axis=1, tiled=True)  29.4 us
    unnamed x16, local copies, waits for them, and re-layouts  5.41 us
  transfers between devices with their start and end apart: 28, of which 14 were waited for; matrix products, arithmetic and copies ran while one was open for 2% of the time, Pallas kernels for 1%

profile of v2, /device:TPU:2, one launch (start us, length us, event | category | flops | bytes accessed | tf_op | source)
XLA Modules:
  0.0 206.0 jit_solution(10245540185895963677)
XLA Ops:
  7.6 1.5 multiply_add_fusion
  9.1 3.3 %modulate.1 = (bf16[96,5120]{1,0:T(8,128)(2,1)}, bf16[64,5120]{1,0:T(8,128)(2,1)}, bf16[32,5120]{1,0:T(8,128)(2,1)}) custom-call(bf16[1,96,5120]{2,1,0:T(8,128)(2,1)} %rows_ref.1, f32[1,5120]{1,0:T(1,128)} %get-tuple-element.12.shift_ref, f32[1,5120]{1,0:T(1,128)} %get-tuple-element.11.scale_ref), custom_call_target="tpu_custom_call" | custom-call | tf_op jit(solution)/shard_map/modulate/pallas_call | solution.py:96
  12.5 2.0 cast_weights.1.refs_1_.refs_9_
  14.5 1.5 collective-permute-start.3
  16.0 7.2 %collective-permute-start = (bf16[64,5120]{1,0:T(8,128)(2,1)}, bf16[64,5120]{1,0:T(8,128)(2,1)S(1)}, u32[]{:S(2)}, u32[]{:S(2)}) collective-permute-start(bf16[64,5120]{1,0:T(8,128)(2,1)} %get-tuple-element.9), channel_id=1, source_target_pairs={{0,8},{1,9},{2,10},{3,11},{4,12},{5,13},{6,14},{7,15},{8,0},{9,1},... | collective-permute-start | bytes 1966088 | tf_op jit(solution)/shard_map/ppermute | solution.py:130
  23.7 4.1 %collective-permute-done.3.refs_0_ = bf16[320,768]{1,0:T(8,128)(2,1)} collective-permute-done((bf16[320,768]{1,0:T(8,128)(2,1)}, bf16[320,768]{1,0:T(8,128)(2,1)}, u32[]{:S(2)}, u32[]{:S(2)}) %collective-permute-start.3) | collective-permute-done | bytes 491552 | tf_op jit(solution)/shard_map/ppermute | solution.py:130
  27.8 1.5 collective-permute-start.4
  29.3 1.9 collective-permute-start.2
  31.2 1.4 collective-permute-start.1
  32.7 3.3 %collective-permute-done.5.refs_0_ = bf16[320,768]{1,0:T(8,128)(2,1)} collective-permute-done((bf16[320,768]{1,0:T(8,128)(2,1)}, bf16[320,768]{1,0:T(8,128)(2,1)}, u32[]{:S(2)}, u32[]{:S(2)}) %collective-permute-start.5) | collective-permute-done | bytes 491552 | tf_op jit(solution)/shard_map/ppermute | solution.py:130
  35.9 4.0 %collective-permute-done.4.refs_0_ = bf16[320,768]{1,0:T(8,128)(2,1)} collective-permute-done((bf16[320,768]{1,0:T(8,128)(2,1)}, bf16[320,768]{1,0:T(8,128)(2,1)}, u32[]{:S(2)}, u32[]{:S(2)}) %collective-permute-start.4) | collective-permute-done | bytes 491552 | tf_op jit(solution)/shard_map/ppermute | solution.py:130
  39.9 23.4 %collective-permute-done.2.refs_0_ = bf16[320,768]{1,0:T(8,128)(2,1)} collective-permute-done((bf16[320,768]{1,0:T(8,128)(2,1)}, bf16[320,768]{1,0:T(8,128)(2,1)}, u32[]{:S(2)}, u32[]{:S(2)}) %collective-permute-start.2) | collective-permute-done | bytes 491552 | tf_op jit(solution)/shard_map/ppermute | solution.py:130
  64.2 1.5 collective-permute-start.6
  69.0 1.3 collective-permute-start.7
  70.3 7.3 %collective-permute-done.10.refs_0_ = bf16[320,768]{1,0:T(8,128)(2,1)S(1)} collective-permute-done((bf16[320,768]{1,0:T(8,128)(2,1)}, bf16[320,768]{1,0:T(8,128)(2,1)S(1)}, u32[]{:S(2)}, u32[]{:S(2)}) %collective-permute-start.10) | collective-permute-done | bytes 491552 | tf_op jit(solution)/shard_map/ppermute | solution.py:130
  79.7 2.1 collective-permute-done.9.refs_0_
  81.7 1.9 broadcast_select_fusion.1.refs_17_
  84.2 1.5 collective-permute-start.12
  86.4 5.7 %collective-permute-done.7.refs_0_ = bf16[320,768]{1,0:T(8,128)(2,1)} collective-permute-done((bf16[320,768]{1,0:T(8,128)(2,1)}, bf16[320,768]{1,0:T(8,128)(2,1)}, u32[]{:S(2)}, u32[]{:S(2)}) %collective-permute-start.7) | collective-permute-done | bytes 491552 | tf_op jit(solution)/shard_map/ppermute | solution.py:130
  92.1 2.4 %collective-permute-start.11 = (bf16[32,5120]{1,0:T(8,128)(2,1)}, bf16[32,5120]{1,0:T(8,128)(2,1)}, u32[]{:S(2)}, u32[]{:S(2)}) collective-permute-start(bf16[32,5120]{1,0:T(8,128)(2,1)} %gate.35.refs_1_), channel_id=1, source_target_pairs={{0,8},{1,9},{2,10},{3,11},{4,12},{5,13},{6,14},{7,15},{8,0},{9,1},... | collective-permute-start | bytes 983048 | tf_op jit(solution)/shard_map/ppermute | solution.py:130
  94.6 1.9 broadcast_select_fusion.refs_21_
  98.5 4.5 %collective-permute-done.13.refs_0_ = bf16[320,768]{1,0:T(8,128)(2,1)} collective-permute-done((bf16[320,768]{1,0:T(8,128)(2,1)}, bf16[320,768]{1,0:T(8,128)(2,1)}, u32[]{:S(2)}, u32[]{:S(2)}) %collective-permute-start.13) | collective-permute-done | bytes 491552 | tf_op jit(solution)/shard_map/ppermute | solution.py:130
  103.0 3.4 %collective-permute-start.16 = (bf16[320,768]{1,0:T(8,128)(2,1)}, bf16[320,768]{1,0:T(8,128)(2,1)}, u32[]{:S(2)}, u32[]{:S(2)}) collective-permute-start(bf16[320,768]{1,0:T(8,128)(2,1)} %gate.38.refs_1_.refs_19_), channel_id=1, source_target_pairs={{0,192},{16,208},{32,224},{48,240},{64,0},{80,16},{96,32},{112,48}... | collective-permute-start | bytes 1474568 | tf_op jit(solution)/shard_map/ppermute | solution.py:130
  106.4 4.7 %collective-permute-done.11.refs_0_ = bf16[32,5120]{1,0:T(8,128)(2,1)} collective-permute-done((bf16[32,5120]{1,0:T(8,128)(2,1)}, bf16[32,5120]{1,0:T(8,128)(2,1)}, u32[]{:S(2)}, u32[]{:S(2)}) %collective-permute-start.11) | collective-permute-done | bytes 327712 | tf_op jit(solution)/shard_map/ppermute | solution.py:130
  111.2 3.0 %collective-permute-start.20 = (bf16[32,5120]{1,0:T(8,128)(2,1)}, bf16[32,5120]{1,0:T(8,128)(2,1)}, u32[]{:S(2)}, u32[]{:S(2)}) collective-permute-start(bf16[32,5120]{1,0:T(8,128)(2,1)} %gate.39.refs_1_), channel_id=1, source_target_pairs={{0,6},{1,7},{2,0},{3,1},{4,2},{5,3},{6,4},{7,5},{8,14},{9,15},{10,... | collective-permute-start | bytes 983048 | tf_op jit(solution)/shard_map/ppermute | solution.py:130
  115.0 4.5 %collective-permute-done.16.refs_0_ = bf16[320,768]{1,0:T(8,128)(2,1)} collective-permute-done((bf16[320,768]{1,0:T(8,128)(2,1)}, bf16[320,768]{1,0:T(8,128)(2,1)}, u32[]{:S(2)}, u32[]{:S(2)}) %collective-permute-start.16) | collective-permute-done | bytes 491552 | tf_op jit(solution)/shard_map/ppermute | solution.py:130
  119.5 2.6 %collective-permute-done.20.refs_0_ = bf16[32,5120]{1,0:T(8,128)(2,1)} collective-permute-done((bf16[32,5120]{1,0:T(8,128)(2,1)}, bf16[32,5120]{1,0:T(8,128)(2,1)}, u32[]{:S(2)}, u32[]{:S(2)}) %collective-permute-start.20) | collective-permute-done | bytes 327712 | tf_op jit(solution)/shard_map/ppermute | solution.py:130
  122.1 3.7 %collective-permute-start.23 = (bf16[32,5120]{1,0:T(8,128)(2,1)}, bf16[32,5120]{1,0:T(8,128)(2,1)S(1)}, u32[]{:S(2)}, u32[]{:S(2)}) collective-permute-start(bf16[32,5120]{1,0:T(8,128)(2,1)} %gate.44.refs_1_.refs_5_), channel_id=1, source_target_pairs={{0,6},{1,7},{2,0},{3,1},{4,2},{5,3},{6,4},{7,5},{8,14},{9,15},{10,... | collective-permute-start | bytes 983048 | tf_op jit(solution)/shard_map/ppermute | solution.py:130
  126.3 1.4 collective-permute-done.24.refs_0_
  128.6 4.5 %collective-permute-done.23.refs_0_ = bf16[32,5120]{1,0:T(8,128)(2,1)S(1)} collective-permute-done((bf16[32,5120]{1,0:T(8,128)(2,1)}, bf16[32,5120]{1,0:T(8,128)(2,1)S(1)}, u32[]{:S(2)}, u32[]{:S(2)}) %collective-permute-start.23) | collective-permute-done | bytes 327712 | tf_op jit(solution)/shard_map/ppermute | solution.py:130
  136.3 31.8 %attend_all.1 = bf16[1536,256]{1,0:T(8,128)(2,1)} custom-call(s32[1]{0:T(128)S(6)} %copy.59.count_ref, s32[33]{0:T(128)} %concatenate.8.place_ref, bf16[768,5120]{1,0:T(8,128)(2,1)} %all-gather.3.cloned.1.call-done.refs_2_.near_ref, bf16[512,5120]{1,0:T(8,128)(2,1)} %all-gather.5.cloned.1.call-done.refs_0_, bf16[32,5120]{1,0:T(8,128)(2,1)} %gate.39.refs_1_, ...), custom_call_target="tpu_custom_call" | custom-call | tf_op jit(solution)/shard_map/attend_all/pallas_call | solution.py:227
  168.1 29.4 %all_to_all.16 = bf16[16,96,256]{2,1,0:T(8,128)(2,1)S(1)} all-to-all(bf16[16,96,256]{2,1,0:T(8,128)(2,1)} %bitcast.28), channel_id=1, replica_groups=mesh['rep'=16,'seq'=16] {'seq'}, dimensions={0} | all-to-all | bytes 1572864 | tf_op jit(solution)/shard_map/all_to_all | solution.py:339
  (77 shorter events, 17.0 us)
Async XLA Ops:
  6.5 85.6 %all-gather.3.cloned.1.call-start = ((), (), s32[]{:S(2)}) async-start(), calls=%async_computation.1 | async-start | bytes 8847360 | tf_op jit(solution)/shard_map/all_gather | solution.py:260
  12.5 122.7 %all-gather.5.cloned.1.call-start = ((), (), s32[]{:S(2)}) async-start(), calls=%async_computation.2 | async-start | bytes 5898240 | tf_op jit(solution)/shard_map/all_gather | solution.py:281
  14.5 13.3 %collective-permute-start.3 = (bf16[320,768]{1,0:T(8,128)(2,1)}, bf16[320,768]{1,0:T(8,128)(2,1)}, u32[]{:S(2)}, u32[]{:S(2)}) collective-permute-start(bf16[320,768]{1,0:T(8,128)(2,1)} %cast_weights.1.refs_1_.refs_9_), channel_id=1, source_target_pairs={{0,64},{16,80},{32,96},{48,112},{64,128},{80,144},{96,160},{112,17... | collective-permute-start | bytes 1474568 | tf_op jit(solution)/shard_map/ppermute | solution.py:130
  16.0 47.3 %collective-permute-start = (bf16[64,5120]{1,0:T(8,128)(2,1)}, bf16[64,5120]{1,0:T(8,128)(2,1)S(1)}, u32[]{:S(2)}, u32[]{:S(2)}) collective-permute-start(bf16[64,5120]{1,0:T(8,128)(2,1)} %get-tuple-element.9), channel_id=1, source_target_pairs={{0,8},{1,9},{2,10},{3,11},{4,12},{5,13},{6,14},{7,15},{8,0},{9,1},... | collective-permute-start | bytes 1966088 | tf_op jit(solution)/shard_map/ppermute | solution.py:130
  23.2 12.7 %collective-permute-start.5 = (bf16[320,768]{1,0:T(8,128)(2,1)}, bf16[320,768]{1,0:T(8,128)(2,1)}, u32[]{:S(2)}, u32[]{:S(2)}) collective-permute-start(bf16[320,768]{1,0:T(8,128)(2,1)} %cast_weights.1.refs_1_.refs_9_), channel_id=1, source_target_pairs={{0,192},{16,208},{32,224},{48,240},{64,0},{80,16},{96,32},{112,48}... | collective-permute-start | bytes 1474568 | tf_op jit(solution)/shard_map/ppermute | solution.py:130
  27.8 12.1 %collective-permute-start.4 = (bf16[320,768]{1,0:T(8,128)(2,1)}, bf16[320,768]{1,0:T(8,128)(2,1)}, u32[]{:S(2)}, u32[]{:S(2)}) collective-permute-start(bf16[320,768]{1,0:T(8,128)(2,1)} %gate.24.refs_1_.refs_10_), channel_id=1, source_target_pairs={{0,64},{16,80},{32,96},{48,112},{64,128},{80,144},{96,160},{112,17... | collective-permute-start | bytes 1474568 | tf_op jit(solution)/shard_map/ppermute | solution.py:130
  29.3 34.0 %collective-permute-start.2 = (bf16[320,768]{1,0:T(8,128)(2,1)}, bf16[320,768]{1,0:T(8,128)(2,1)}, u32[]{:S(2)}, u32[]{:S(2)}) collective-permute-start(bf16[320,768]{1,0:T(8,128)(2,1)} %cast_weights.1.refs_1_.refs_9_), channel_id=1, source_target_pairs={{0,16},{16,0},{32,48},{48,32},{64,80},{80,64},{96,112},{112,96},{1... | collective-permute-start | bytes 1474568 | tf_op jit(solution)/shard_map/ppermute | solution.py:130
  31.2 32.1 %collective-permute-start.1 = (bf16[320,768]{1,0:T(8,128)(2,1)}, bf16[320,768]{1,0:T(8,128)(2,1)}, u32[]{:S(2)}, u32[]{:S(2)}) collective-permute-start(bf16[320,768]{1,0:T(8,128)(2,1)} %cast_weights.1.refs_1_.refs_9_), channel_id=1, source_target_pairs={{16,32},{32,16},{80,96},{96,80},{144,160},{160,144},{208,224},{224... | collective-permute-start | bytes 1474568 | tf_op jit(solution)/shard_map/ppermute | solution.py:130
  63.3 0.8 copy-start
  64.2 4.9 %collective-permute-start.6 = (bf16[320,768]{1,0:T(8,128)(2,1)}, bf16[320,768]{1,0:T(8,128)(2,1)}, u32[]{:S(2)}, u32[]{:S(2)}) collective-permute-start(bf16[320,768]{1,0:T(8,128)(2,1)} %gate.27.refs_1_.refs_13_), channel_id=1, source_target_pairs={{16,32},{32,16},{80,96},{96,80},{144,160},{160,144},{208,224},{224... | collective-permute-start | bytes 1474568 | tf_op jit(solution)/shard_map/ppermute | solution.py:130
  65.6 12.0 %collective-permute-start.10 = (bf16[320,768]{1,0:T(8,128)(2,1)}, bf16[320,768]{1,0:T(8,128)(2,1)S(1)}, u32[]{:S(2)}, u32[]{:S(2)}) collective-permute-start(bf16[320,768]{1,0:T(8,128)(2,1)} %gate.27.refs_1_.refs_13_), channel_id=1, source_target_pairs={{0,64},{16,80},{32,96},{48,112},{64,128},{80,144},{96,160},{112,17... | collective-permute-start | bytes 1474568 | tf_op jit(solution)/shard_map/ppermute | solution.py:130
  66.8 14.9 %collective-permute-start.9 = (bf16[320,768]{1,0:T(8,128)(2,1)}, bf16[320,768]{1,0:T(8,128)(2,1)}, u32[]{:S(2)}, u32[]{:S(2)}) collective-permute-start(bf16[320,768]{1,0:T(8,128)(2,1)} %gate.28.refs_1_), channel_id=1, source_target_pairs={{16,0},{32,48},{80,64},{96,112},{144,128},{160,176},{208,192},{224... | collective-permute-start | bytes 1474568 | tf_op jit(solution)/shard_map/ppermute | solution.py:130
  68.1 17.5 %collective-permute-start.8 = (bf16[320,768]{1,0:T(8,128)(2,1)}, bf16[320,768]{1,0:T(8,128)(2,1)S(1)}, u32[]{:S(2)}, u32[]{:S(2)}) collective-permute-start(bf16[320,768]{1,0:T(8,128)(2,1)} %gate.27.refs_1_.refs_13_), channel_id=1, source_target_pairs={{0,192},{16,208},{32,224},{48,240},{64,0},{80,16},{96,32},{112,48}... | collective-permute-start | bytes 1474568 | tf_op jit(solution)/shard_map/ppermute | solution.py:130
  69.0 23.1 %collective-permute-start.7 = (bf16[320,768]{1,0:T(8,128)(2,1)}, bf16[320,768]{1,0:T(8,128)(2,1)}, u32[]{:S(2)}, u32[]{:S(2)}) collective-permute-start(bf16[320,768]{1,0:T(8,128)(2,1)} %gate.30.refs_1_), channel_id=1, source_target_pairs={{16,0},{32,48},{80,64},{96,112},{144,128},{160,176},{208,192},{224... | collective-permute-start | bytes 1474568 | tf_op jit(solution)/shard_map/ppermute | solution.py:130
  78.5 19.2 %collective-permute-start.14 = (bf16[320,768]{1,0:T(8,128)(2,1)}, bf16[320,768]{1,0:T(8,128)(2,1)S(1)}, u32[]{:S(2)}, u32[]{:S(2)}) collective-permute-start(bf16[320,768]{1,0:T(8,128)(2,1)} %gate.31.refs_1_.refs_14_), channel_id=1, source_target_pairs={{0,64},{16,80},{32,96},{48,112},{64,128},{80,144},{96,160},{112,17... | collective-permute-start | bytes 1474568 | tf_op jit(solution)/shard_map/ppermute | solution.py:130
  83.6 19.4 %collective-permute-start.13 = (bf16[320,768]{1,0:T(8,128)(2,1)}, bf16[320,768]{1,0:T(8,128)(2,1)}, u32[]{:S(2)}, u32[]{:S(2)}) collective-permute-start(bf16[320,768]{1,0:T(8,128)(2,1)} %broadcast_select_fusion.1.refs_17_), channel_id=1, source_target_pairs={{0,64},{16,80},{32,96},{48,112},{64,128},{80,144},{96,160},{112,17... | collective-permute-start | bytes 1474568 | tf_op jit(solution)/shard_map/ppermute | solution.py:130
  84.2 18.8 %collective-permute-start.12 = (bf16[320,768]{1,0:T(8,128)(2,1)}, bf16[320,768]{1,0:T(8,128)(2,1)}, u32[]{:S(2)}, u32[]{:S(2)}) collective-permute-start(bf16[320,768]{1,0:T(8,128)(2,1)} %broadcast_select_fusion.1.refs_17_), channel_id=1, source_target_pairs={{0,192},{16,208},{32,224},{48,240},{64,0},{80,16},{96,32},{112,48}... | collective-permute-start | bytes 1474568 | tf_op jit(solution)/shard_map/ppermute | solution.py:130
  85.6 0.8 copy-start.1
  92.1 19.0 %collective-permute-start.11 = (bf16[32,5120]{1,0:T(8,128)(2,1)}, bf16[32,5120]{1,0:T(8,128)(2,1)}, u32[]{:S(2)}, u32[]{:S(2)}) collective-permute-start(bf16[32,5120]{1,0:T(8,128)(2,1)} %gate.35.refs_1_), channel_id=1, source_target_pairs={{0,8},{1,9},{2,10},{3,11},{4,12},{5,13},{6,14},{7,15},{8,0},{9,1},... | collective-permute-start | bytes 983048 | tf_op jit(solution)/shard_map/ppermute | solution.py:130
  96.4 17.8 %collective-permute-start.18 = (bf16[320,768]{1,0:T(8,128)(2,1)}, bf16[320,768]{1,0:T(8,128)(2,1)}, u32[]{:S(2)}, u32[]{:S(2)}) collective-permute-start(bf16[320,768]{1,0:T(8,128)(2,1)} %broadcast_select_fusion.refs_21_), channel_id=1, source_target_pairs={{0,64},{16,80},{32,96},{48,112},{64,128},{80,144},{96,160},{112,17... | collective-permute-start | bytes 1474568 | tf_op jit(solution)/shard_map/ppermute | solution.py:130
  97.6 0.8 copy-start.2
  97.6 16.6 %collective-permute-start.17 = (bf16[320,768]{1,0:T(8,128)(2,1)}, bf16[320,768]{1,0:T(8,128)(2,1)S(1)}, u32[]{:S(2)}, u32[]{:S(2)}) collective-permute-start(bf16[320,768]{1,0:T(8,128)(2,1)} %broadcast_select_fusion.refs_21_), channel_id=1, source_target_pairs={{0,192},{16,208},{32,224},{48,240},{64,0},{80,16},{96,32},{112,48}... | collective-permute-start | bytes 1474568 | tf_op jit(solution)/shard_map/ppermute | solution.py:130
  103.0 16.5 %collective-permute-start.16 = (bf16[320,768]{1,0:T(8,128)(2,1)}, bf16[320,768]{1,0:T(8,128)(2,1)}, u32[]{:S(2)}, u32[]{:S(2)}) collective-permute-start(bf16[320,768]{1,0:T(8,128)(2,1)} %gate.38.refs_1_.refs_19_), channel_id=1, source_target_pairs={{0,192},{16,208},{32,224},{48,240},{64,0},{80,16},{96,32},{112,48}... | collective-permute-start | bytes 1474568 | tf_op jit(solution)/shard_map/ppermute | solution.py:130
  111.2 8.4 %collective-permute-start.15 = (bf16[32,5120]{1,0:T(8,128)(2,1)}, bf16[32,5120]{1,0:T(8,128)(2,1)}, u32[]{:S(2)}, u32[]{:S(2)}) collective-permute-start(bf16[32,5120]{1,0:T(8,128)(2,1)} %gate.39.refs_1_), channel_id=1, source_target_pairs={{0,1},{1,0},{2,3},{3,2},{4,5},{5,4},{6,7},{7,6},{8,9},{9,8},{10,11... | collective-permute-start | bytes 983048 | tf_op jit(solution)/shard_map/ppermute | solution.py:130
  111.2 11.0 %collective-permute-start.20 = (bf16[32,5120]{1,0:T(8,128)(2,1)}, bf16[32,5120]{1,0:T(8,128)(2,1)}, u32[]{:S(2)}, u32[]{:S(2)}) collective-permute-start(bf16[32,5120]{1,0:T(8,128)(2,1)} %gate.39.refs_1_), channel_id=1, source_target_pairs={{0,6},{1,7},{2,0},{3,1},{4,2},{5,3},{6,4},{7,5},{8,14},{9,15},{10,... | collective-permute-start | bytes 983048 | tf_op jit(solution)/shard_map/ppermute | solution.py:130
  114.2 13.6 %collective-permute-start.24 = (bf16[320,768]{1,0:T(8,128)(2,1)}, bf16[320,768]{1,0:T(8,128)(2,1)S(1)}, u32[]{:S(2)}, u32[]{:S(2)}) collective-permute-start(bf16[320,768]{1,0:T(8,128)(2,1)} %gate.40.refs_1_.refs_22_), channel_id=1, source_target_pairs={{0,64},{16,80},{32,96},{48,112},{64,128},{80,144},{96,160},{112,17... | collective-permute-start | bytes 1474568 | tf_op jit(solution)/shard_map/ppermute | solution.py:130
  114.2 11.6 %collective-permute-start.19 = (bf16[32,5120]{1,0:T(8,128)(2,1)}, bf16[32,5120]{1,0:T(8,128)(2,1)}, u32[]{:S(2)}, u32[]{:S(2)}) collective-permute-start(bf16[32,5120]{1,0:T(8,128)(2,1)} %gate.39.refs_1_), channel_id=1, source_target_pairs={{0,2},{1,3},{2,4},{3,5},{4,6},{5,7},{6,0},{7,1},{8,10},{9,11},{10,... | collective-permute-start | bytes 983048 | tf_op jit(solution)/shard_map/ppermute | solution.py:130
  122.1 10.9 %collective-permute-start.23 = (bf16[32,5120]{1,0:T(8,128)(2,1)}, bf16[32,5120]{1,0:T(8,128)(2,1)S(1)}, u32[]{:S(2)}, u32[]{:S(2)}) collective-permute-start(bf16[32,5120]{1,0:T(8,128)(2,1)} %gate.44.refs_1_.refs_5_), channel_id=1, source_target_pairs={{0,6},{1,7},{2,0},{3,1},{4,2},{5,3},{6,4},{7,5},{8,14},{9,15},{10,... | collective-permute-start | bytes 983048 | tf_op jit(solution)/shard_map/ppermute | solution.py:130
  125.8 9.3 %collective-permute-start.22 = (bf16[32,5120]{1,0:T(8,128)(2,1)}, bf16[32,5120]{1,0:T(8,128)(2,1)}, u32[]{:S(2)}, u32[]{:S(2)}) collective-permute-start(bf16[32,5120]{1,0:T(8,128)(2,1)} %gate.44.refs_1_.refs_5_), channel_id=1, source_target_pairs={{0,1},{1,0},{2,3},{3,2},{4,5},{5,4},{6,7},{7,6},{8,9},{9,8},{10,11... | collective-permute-start | bytes 983048 | tf_op jit(solution)/shard_map/ppermute | solution.py:130
  125.8 9.3 %collective-permute-start.21 = (bf16[32,5120]{1,0:T(8,128)(2,1)}, bf16[32,5120]{1,0:T(8,128)(2,1)}, u32[]{:S(2)}, u32[]{:S(2)}) collective-permute-start(bf16[32,5120]{1,0:T(8,128)(2,1)} %gate.45.refs_1_.refs_3_), channel_id=1, source_target_pairs={{0,1},{1,0},{2,3},{3,2},{4,5},{5,4},{6,7},{7,6},{8,9},{9,8},{10,11... | collective-permute-start | bytes 983048 | tf_op jit(solution)/shard_map/ppermute | solution.py:130
  127.8 0.8 copy-start.5
  133.7 1.8 collective-permute-start.25
  (4 other events, 3.0 us)
Sparse Core Ops, SparseCore 0:
  12.6 53.0 all-gather.2
  67.5 39.2 all-gather.4

commit v3 on v2

--- a/solution.py
+++ b/solution.py
@@ -50,14 +50,13 @@
 C_SWAP = seq_perm(lambda h, y, c: (h, y, 1 - c))
 
 
-def modulation(step_value, mod_base, mod_time, width):
+def time_embedding(step_value, width):
     frac = 1.0 - step_value.astype(jnp.float32) / STEPS
     sigma = 5.0 * frac / (1.0 + 4.0 * frac)
     half_width = width // 2
     freqs = jnp.exp(-math.log(10000.0) * jnp.arange(half_width, dtype=jnp.float32) / half_width)
     angles = 1000.0 * sigma * freqs
-    embedding = jnp.concatenate([jnp.cos(angles), jnp.sin(angles)])
-    return (mod_base[0] + mod_time[0] * embedding, mod_base[1] + mod_time[1] * embedding)
+    return jnp.concatenate([jnp.cos(angles), jnp.sin(angles)])
 
 
 def cast_kernel(q_ref, k_ref, v_ref, before_ref, out_ref):
@@ -78,20 +77,23 @@
     )(w_query, w_key, w_value, before)
 
 
-def modulate_kernel(rows_ref, shift_ref, scale_ref, all_ref, early_ref, late_ref):
+def modulate_kernel(rows_ref, base_ref, time_ref, embedding_ref, all_ref, early_ref, late_ref):
+    embedding = embedding_ref[...]
+    shift = base_ref[0:1, :] + time_ref[0:1, :] * embedding
+    scale = base_ref[1:2, :] + time_ref[1:2, :] * embedding
     values = rows_ref[0].astype(jnp.float32)
     center = jnp.mean(values, axis=1, keepdims=True)
     moved = values - center
     spread = jnp.mean(moved * moved, axis=1, keepdims=True)
     normed = moved * lax.rsqrt(spread + 1e-06)
-    result = (normed * (1.0 + scale_ref[...]) + shift_ref[...]).astype(jnp.bfloat16)
+    result = (normed * (1.0 + scale) + shift).astype(jnp.bfloat16)
     early = early_ref.shape[0]
     all_ref[...] = result
     early_ref[...] = result[:early]
     late_ref[...] = result[early:]
 
 
-def modulate(tokens, shift_row, scale_row, early):
+def modulate(tokens, mod_base, mod_time, embedding, early):
     _, rows, width = tokens.shape
     return pl.pallas_call(
         modulate_kernel,
@@ -99,7 +101,7 @@
             jax.ShapeDtypeStruct((count, width), jnp.bfloat16) for count in (rows, early, rows - early)
         ),
         name="modulate",
-    )(tokens, shift_row[None], scale_row[None])
+    )(tokens, mod_base, mod_time, embedding[None])
 
 
 def gate_kernel(*refs):
@@ -254,8 +256,8 @@
 
     rows = tokens.shape[1]
     early, late = EARLY, rows - EARLY
-    shift_row, scale_row = modulation(steps[0], mod_base, mod_time, width)
-    mine, t0, t1 = modulate(tokens, shift_row, scale_row, early)
+    embedding = time_embedding(steps[0], width)
+    mine, t0, t1 = modulate(tokens, mod_base, mod_time, embedding, early)
     groups = [[(h * NY + y) * NC + c for y in range(NY) for c in range(NC)] for h in range(2)]
     near = lax.all_gather(mine, "seq", axis=0, axis_index_groups=groups, tiled=True)
     own = cast_weights(w_query, w_key, w_value, mine)

time: 206 us -> 205 us (level)
  no operation moved by 1% of the time
where the time goes in v3:
time: 205 us
  waiting for transfers between devices  72.6 us (35%)
  starting transfers between devices  38.6 us (19%)
  Pallas kernels  37.2 us (18%)
  blocking collectives  29.4 us (14%)
  between operations  14.9 us (7%)
  local copies, waits for them, and re-layouts  7.78 us (4%)
  other arithmetic  4.42 us (2%)
    ppermute x26, waiting for transfers between devices, start(): self.flying[name] = lax.ppermute(array, axis, perm)  72.6 us
    ppermute x26, starting transfers between devices, start(): self.flying[name] = lax.ppermute(array, axis, perm)  38.6 us
    pallas_call x1, Pallas kernels, attend_all(): pl.pallas_call(functools.partial(attend_kernel, heads=heads, pieces=piece...  31.8 us
    all_to_all x1, blocking collectives, shards(): lax.all_to_all(head_output, 'seq', split_axis=0, concat_axis=1, tiled=True)  29.4 us
    unnamed x16, local copies, waits for them, and re-layouts  5.44 us
  transfers between devices with their start and end apart: 28, of which 14 were waited for; matrix products, arithmetic and copies ran while one was open for 2% of the time, Pallas kernels for 1%

profile of v3, /device:TPU:2, one launch (start us, length us, event | category | flops | bytes accessed | tf_op | source)
XLA Modules:
  0.0 204.8 jit_solution(5807017613926798576)
XLA Ops:
  7.9 3.3 %modulate.1 = (bf16[96,5120]{1,0:T(8,128)(2,1)}, bf16[64,5120]{1,0:T(8,128)(2,1)}, bf16[32,5120]{1,0:T(8,128)(2,1)}) custom-call(bf16[1,96,5120]{2,1,0:T(8,128)(2,1)} %rows_ref.1, f32[2,5120]{1,0:T(2,128)} %base_ref.1, f32[2,5120]{1,0:T(2,128)} %time_ref.1, f32[1,5120]{1,0:T(1,128)} %bitcast.31), custom_call_target="tpu_custom_call" | custom-call | tf_op jit(solution)/shard_map/modulate/pallas_call | solution.py:98
  11.3 2.0 cast_weights.1.refs_1_.refs_9_
  13.3 1.5 collective-permute-start.3
  14.8 7.2 %collective-permute-start = (bf16[64,5120]{1,0:T(8,128)(2,1)}, bf16[64,5120]{1,0:T(8,128)(2,1)S(1)}, u32[]{:S(2)}, u32[]{:S(2)}) collective-permute-start(bf16[64,5120]{1,0:T(8,128)(2,1)} %get-tuple-element.9), channel_id=1, source_target_pairs={{0,8},{1,9},{2,10},{3,11},{4,12},{5,13},{6,14},{7,15},{8,0},{9,1},... | collective-permute-start | bytes 1966088 | tf_op jit(solution)/shard_map/ppermute | solution.py:132
  22.6 4.1 %collective-permute-done.3.refs_0_ = bf16[320,768]{1,0:T(8,128)(2,1)} collective-permute-done((bf16[320,768]{1,0:T(8,128)(2,1)}, bf16[320,768]{1,0:T(8,128)(2,1)}, u32[]{:S(2)}, u32[]{:S(2)}) %collective-permute-start.3) | collective-permute-done | bytes 491552 | tf_op jit(solution)/shard_map/ppermute | solution.py:132
  26.6 1.5 collective-permute-start.4
  28.1 1.9 collective-permute-start.2
  30.0 1.4 collective-permute-start.1
  31.5 3.3 %collective-permute-done.5.refs_0_ = bf16[320,768]{1,0:T(8,128)(2,1)} collective-permute-done((bf16[320,768]{1,0:T(8,128)(2,1)}, bf16[320,768]{1,0:T(8,128)(2,1)}, u32[]{:S(2)}, u32[]{:S(2)}) %collective-permute-start.5) | collective-permute-done | bytes 491552 | tf_op jit(solution)/shard_map/ppermute | solution.py:132
  34.7 4.0 %collective-permute-done.4.refs_0_ = bf16[320,768]{1,0:T(8,128)(2,1)} collective-permute-done((bf16[320,768]{1,0:T(8,128)(2,1)}, bf16[320,768]{1,0:T(8,128)(2,1)}, u32[]{:S(2)}, u32[]{:S(2)}) %collective-permute-start.4) | collective-permute-done | bytes 491552 | tf_op jit(solution)/shard_map/ppermute | solution.py:132
  38.7 23.4 %collective-permute-done.2.refs_0_ = bf16[320,768]{1,0:T(8,128)(2,1)} collective-permute-done((bf16[320,768]{1,0:T(8,128)(2,1)}, bf16[320,768]{1,0:T(8,128)(2,1)}, u32[]{:S(2)}, u32[]{:S(2)}) %collective-permute-start.2) | collective-permute-done | bytes 491552 | tf_op jit(solution)/shard_map/ppermute | solution.py:132
  63.0 1.5 collective-permute-start.6
  65.7 1.3 collective-permute-start.9
  67.9 1.3 collective-permute-start.7
  69.2 7.3 %collective-permute-done.10.refs_0_ = bf16[320,768]{1,0:T(8,128)(2,1)S(1)} collective-permute-done((bf16[320,768]{1,0:T(8,128)(2,1)}, bf16[320,768]{1,0:T(8,128)(2,1)S(1)}, u32[]{:S(2)}, u32[]{:S(2)}) %collective-permute-start.10) | collective-permute-done | bytes 491552 | tf_op jit(solution)/shard_map/ppermute | solution.py:132
  78.5 2.0 collective-permute-done.9.refs_0_
  80.5 1.9 broadcast_select_fusion.1.refs_17_
  83.0 1.5 collective-permute-start.12
  85.2 5.7 %collective-permute-done.7.refs_0_ = bf16[320,768]{1,0:T(8,128)(2,1)} collective-permute-done((bf16[320,768]{1,0:T(8,128)(2,1)}, bf16[320,768]{1,0:T(8,128)(2,1)}, u32[]{:S(2)}, u32[]{:S(2)}) %collective-permute-start.7) | collective-permute-done | bytes 491552 | tf_op jit(solution)/shard_map/ppermute | solution.py:132
  91.0 2.4 %collective-permute-start.11 = (bf16[32,5120]{1,0:T(8,128)(2,1)}, bf16[32,5120]{1,0:T(8,128)(2,1)}, u32[]{:S(2)}, u32[]{:S(2)}) collective-permute-start(bf16[32,5120]{1,0:T(8,128)(2,1)} %gate.35.refs_1_), channel_id=1, source_target_pairs={{0,8},{1,9},{2,10},{3,11},{4,12},{5,13},{6,14},{7,15},{8,0},{9,1},... | collective-permute-start | bytes 983048 | tf_op jit(solution)/shard_map/ppermute | solution.py:132
  93.4 1.9 broadcast_select_fusion.refs_21_
  97.3 4.6 %collective-permute-done.13.refs_0_ = bf16[320,768]{1,0:T(8,128)(2,1)} collective-permute-done((bf16[320,768]{1,0:T(8,128)(2,1)}, bf16[320,768]{1,0:T(8,128)(2,1)}, u32[]{:S(2)}, u32[]{:S(2)}) %collective-permute-start.13) | collective-permute-done | bytes 491552 | tf_op jit(solution)/shard_map/ppermute | solution.py:132
  101.9 3.4 %collective-permute-start.16 = (bf16[320,768]{1,0:T(8,128)(2,1)}, bf16[320,768]{1,0:T(8,128)(2,1)}, u32[]{:S(2)}, u32[]{:S(2)}) collective-permute-start(bf16[320,768]{1,0:T(8,128)(2,1)} %gate.38.refs_1_.refs_19_), channel_id=1, source_target_pairs={{0,192},{16,208},{32,224},{48,240},{64,0},{80,16},{96,32},{112,48}... | collective-permute-start | bytes 1474568 | tf_op jit(solution)/shard_map/ppermute | solution.py:132
  105.2 4.7 %collective-permute-done.11.refs_0_ = bf16[32,5120]{1,0:T(8,128)(2,1)} collective-permute-done((bf16[32,5120]{1,0:T(8,128)(2,1)}, bf16[32,5120]{1,0:T(8,128)(2,1)}, u32[]{:S(2)}, u32[]{:S(2)}) %collective-permute-start.11) | collective-permute-done | bytes 327712 | tf_op jit(solution)/shard_map/ppermute | solution.py:132
  110.0 3.0 %collective-permute-start.20 = (bf16[32,5120]{1,0:T(8,128)(2,1)}, bf16[32,5120]{1,0:T(8,128)(2,1)}, u32[]{:S(2)}, u32[]{:S(2)}) collective-permute-start(bf16[32,5120]{1,0:T(8,128)(2,1)} %gate.39.refs_1_), channel_id=1, source_target_pairs={{0,6},{1,7},{2,0},{3,1},{4,2},{5,3},{6,4},{7,5},{8,14},{9,15},{10,... | collective-permute-start | bytes 983048 | tf_op jit(solution)/shard_map/ppermute | solution.py:132
  113.8 4.5 %collective-permute-done.16.refs_0_ = bf16[320,768]{1,0:T(8,128)(2,1)} collective-permute-done((bf16[320,768]{1,0:T(8,128)(2,1)}, bf16[320,768]{1,0:T(8,128)(2,1)}, u32[]{:S(2)}, u32[]{:S(2)}) %collective-permute-start.16) | collective-permute-done | bytes 491552 | tf_op jit(solution)/shard_map/ppermute | solution.py:132
  118.3 2.6 %collective-permute-done.20.refs_0_ = bf16[32,5120]{1,0:T(8,128)(2,1)} collective-permute-done((bf16[32,5120]{1,0:T(8,128)(2,1)}, bf16[32,5120]{1,0:T(8,128)(2,1)}, u32[]{:S(2)}, u32[]{:S(2)}) %collective-permute-start.20) | collective-permute-done | bytes 327712 | tf_op jit(solution)/shard_map/ppermute | solution.py:132
  121.0 3.7 %collective-permute-start.23 = (bf16[32,5120]{1,0:T(8,128)(2,1)}, bf16[32,5120]{1,0:T(8,128)(2,1)S(1)}, u32[]{:S(2)}, u32[]{:S(2)}) collective-permute-start(bf16[32,5120]{1,0:T(8,128)(2,1)} %gate.44.refs_1_.refs_5_), channel_id=1, source_target_pairs={{0,6},{1,7},{2,0},{3,1},{4,2},{5,3},{6,4},{7,5},{8,14},{9,15},{10,... | collective-permute-start | bytes 983048 | tf_op jit(solution)/shard_map/ppermute | solution.py:132
  125.2 1.4 collective-permute-done.24.refs_0_
  127.4 4.5 %collective-permute-done.23.refs_0_ = bf16[32,5120]{1,0:T(8,128)(2,1)S(1)} collective-permute-done((bf16[32,5120]{1,0:T(8,128)(2,1)}, bf16[32,5120]{1,0:T(8,128)(2,1)S(1)}, u32[]{:S(2)}, u32[]{:S(2)}) %collective-permute-start.23) | collective-permute-done | bytes 327712 | tf_op jit(solution)/shard_map/ppermute | solution.py:132
  135.2 31.8 %attend_all.1 = bf16[1536,256]{1,0:T(8,128)(2,1)} custom-call(s32[1]{0:T(128)S(6)} %copy.59.count_ref, s32[33]{0:T(128)} %concatenate.6.place_ref, bf16[768,5120]{1,0:T(8,128)(2,1)} %all-gather.3.cloned.1.call-done.refs_2_.near_ref, bf16[512,5120]{1,0:T(8,128)(2,1)} %all-gather.5.cloned.1.call-done.refs_0_, bf16[32,5120]{1,0:T(8,128)(2,1)} %gate.39.refs_1_, ...), custom_call_target="tpu_custom_call" | custom-call | tf_op jit(solution)/shard_map/attend_all/pallas_call | solution.py:229
  167.0 29.4 %all_to_all.16 = bf16[16,96,256]{2,1,0:T(8,128)(2,1)S(1)} all-to-all(bf16[16,96,256]{2,1,0:T(8,128)(2,1)} %bitcast.29), channel_id=1, replica_groups=mesh['rep'=16,'seq'=16] {'seq'}, dimensions={0} | all-to-all | bytes 1572864 | tf_op jit(solution)/shard_map/all_to_all | solution.py:341
  (77 shorter events, 16.1 us)
Async XLA Ops:
  6.5 84.4 %all-gather.3.cloned.1.call-start = ((), (), s32[]{:S(2)}) async-start(), calls=%async_computation.1 | async-start | bytes 8847360 | tf_op jit(solution)/shard_map/all_gather | solution.py:262
  11.3 122.6 %all-gather.5.cloned.1.call-start = ((), (), s32[]{:S(2)}) async-start(), calls=%async_computation.2 | async-start | bytes 5898240 | tf_op jit(solution)/shard_map/all_gather | solution.py:283
  13.3 13.3 %collective-permute-start.3 = (bf16[320,768]{1,0:T(8,128)(2,1)}, bf16[320,768]{1,0:T(8,128)(2,1)}, u32[]{:S(2)}, u32[]{:S(2)}) collective-permute-start(bf16[320,768]{1,0:T(8,128)(2,1)} %cast_weights.1.refs_1_.refs_9_), channel_id=1, source_target_pairs={{0,64},{16,80},{32,96},{48,112},{64,128},{80,144},{96,160},{112,17... | collective-permute-start | bytes 1474568 | tf_op jit(solution)/shard_map/ppermute | solution.py:132
  14.8 47.3 %collective-permute-start = (bf16[64,5120]{1,0:T(8,128)(2,1)}, bf16[64,5120]{1,0:T(8,128)(2,1)S(1)}, u32[]{:S(2)}, u32[]{:S(2)}) collective-permute-start(bf16[64,5120]{1,0:T(8,128)(2,1)} %get-tuple-element.9), channel_id=1, source_target_pairs={{0,8},{1,9},{2,10},{3,11},{4,12},{5,13},{6,14},{7,15},{8,0},{9,1},... | collective-permute-start | bytes 1966088 | tf_op jit(solution)/shard_map/ppermute | solution.py:132
  22.0 12.7 %collective-permute-start.5 = (bf16[320,768]{1,0:T(8,128)(2,1)}, bf16[320,768]{1,0:T(8,128)(2,1)}, u32[]{:S(2)}, u32[]{:S(2)}) collective-permute-start(bf16[320,768]{1,0:T(8,128)(2,1)} %cast_weights.1.refs_1_.refs_9_), channel_id=1, source_target_pairs={{0,192},{16,208},{32,224},{48,240},{64,0},{80,16},{96,32},{112,48}... | collective-permute-start | bytes 1474568 | tf_op jit(solution)/shard_map/ppermute | solution.py:132
  26.6 12.1 %collective-permute-start.4 = (bf16[320,768]{1,0:T(8,128)(2,1)}, bf16[320,768]{1,0:T(8,128)(2,1)}, u32[]{:S(2)}, u32[]{:S(2)}) collective-permute-start(bf16[320,768]{1,0:T(8,128)(2,1)} %gate.24.refs_1_.refs_10_), channel_id=1, source_target_pairs={{0,64},{16,80},{32,96},{48,112},{64,128},{80,144},{96,160},{112,17... | collective-permute-start | bytes 1474568 | tf_op jit(solution)/shard_map/ppermute | solution.py:132
  28.1 34.0 %collective-permute-start.2 = (bf16[320,768]{1,0:T(8,128)(2,1)}, bf16[320,768]{1,0:T(8,128)(2,1)}, u32[]{:S(2)}, u32[]{:S(2)}) collective-permute-start(bf16[320,768]{1,0:T(8,128)(2,1)} %cast_weights.1.refs_1_.refs_9_), channel_id=1, source_target_pairs={{0,16},{16,0},{32,48},{48,32},{64,80},{80,64},{96,112},{112,96},{1... | collective-permute-start | bytes 1474568 | tf_op jit(solution)/shard_map/ppermute | solution.py:132
  30.0 32.1 %collective-permute-start.1 = (bf16[320,768]{1,0:T(8,128)(2,1)}, bf16[320,768]{1,0:T(8,128)(2,1)}, u32[]{:S(2)}, u32[]{:S(2)}) collective-permute-start(bf16[320,768]{1,0:T(8,128)(2,1)} %cast_weights.1.refs_1_.refs_9_), channel_id=1, source_target_pairs={{16,32},{32,16},{80,96},{96,80},{144,160},{160,144},{208,224},{224... | collective-permute-start | bytes 1474568 | tf_op jit(solution)/shard_map/ppermute | solution.py:132
  62.1 0.8 copy-start
  63.0 4.9 %collective-permute-start.6 = (bf16[320,768]{1,0:T(8,128)(2,1)}, bf16[320,768]{1,0:T(8,128)(2,1)}, u32[]{:S(2)}, u32[]{:S(2)}) collective-permute-start(bf16[320,768]{1,0:T(8,128)(2,1)} %gate.27.refs_1_.refs_13_), channel_id=1, source_target_pairs={{16,32},{32,16},{80,96},{96,80},{144,160},{160,144},{208,224},{224... | collective-permute-start | bytes 1474568 | tf_op jit(solution)/shard_map/ppermute | solution.py:132
  64.5 12.0 %collective-permute-start.10 = (bf16[320,768]{1,0:T(8,128)(2,1)}, bf16[320,768]{1,0:T(8,128)(2,1)S(1)}, u32[]{:S(2)}, u32[]{:S(2)}) collective-permute-start(bf16[320,768]{1,0:T(8,128)(2,1)} %gate.27.refs_1_.refs_13_), channel_id=1, source_target_pairs={{0,64},{16,80},{32,96},{48,112},{64,128},{80,144},{96,160},{112,17... | collective-permute-start | bytes 1474568 | tf_op jit(solution)/shard_map/ppermute | solution.py:132
  65.7 14.9 %collective-permute-start.9 = (bf16[320,768]{1,0:T(8,128)(2,1)}, bf16[320,768]{1,0:T(8,128)(2,1)}, u32[]{:S(2)}, u32[]{:S(2)}) collective-permute-start(bf16[320,768]{1,0:T(8,128)(2,1)} %gate.28.refs_1_), channel_id=1, source_target_pairs={{16,0},{32,48},{80,64},{96,112},{144,128},{160,176},{208,192},{224... | collective-permute-start | bytes 1474568 | tf_op jit(solution)/shard_map/ppermute | solution.py:132
  66.9 17.5 %collective-permute-start.8 = (bf16[320,768]{1,0:T(8,128)(2,1)}, bf16[320,768]{1,0:T(8,128)(2,1)S(1)}, u32[]{:S(2)}, u32[]{:S(2)}) collective-permute-start(bf16[320,768]{1,0:T(8,128)(2,1)} %gate.27.refs_1_.refs_13_), channel_id=1, source_target_pairs={{0,192},{16,208},{32,224},{48,240},{64,0},{80,16},{96,32},{112,48}... | collective-permute-start | bytes 1474568 | tf_op jit(solution)/shard_map/ppermute | solution.py:132
  67.9 23.1 %collective-permute-start.7 = (bf16[320,768]{1,0:T(8,128)(2,1)}, bf16[320,768]{1,0:T(8,128)(2,1)}, u32[]{:S(2)}, u32[]{:S(2)}) collective-permute-start(bf16[320,768]{1,0:T(8,128)(2,1)} %gate.30.refs_1_), channel_id=1, source_target_pairs={{16,0},{32,48},{80,64},{96,112},{144,128},{160,176},{208,192},{224... | collective-permute-start | bytes 1474568 | tf_op jit(solution)/shard_map/ppermute | solution.py:132
  77.3 19.2 %collective-permute-start.14 = (bf16[320,768]{1,0:T(8,128)(2,1)}, bf16[320,768]{1,0:T(8,128)(2,1)S(1)}, u32[]{:S(2)}, u32[]{:S(2)}) collective-permute-start(bf16[320,768]{1,0:T(8,128)(2,1)} %gate.31.refs_1_.refs_14_), channel_id=1, source_target_pairs={{0,64},{16,80},{32,96},{48,112},{64,128},{80,144},{96,160},{112,17... | collective-permute-start | bytes 1474568 | tf_op jit(solution)/shard_map/ppermute | solution.py:132
  82.4 19.4 %collective-permute-start.13 = (bf16[320,768]{1,0:T(8,128)(2,1)}, bf16[320,768]{1,0:T(8,128)(2,1)}, u32[]{:S(2)}, u32[]{:S(2)}) collective-permute-start(bf16[320,768]{1,0:T(8,128)(2,1)} %broadcast_select_fusion.1.refs_17_), channel_id=1, source_target_pairs={{0,64},{16,80},{32,96},{48,112},{64,128},{80,144},{96,160},{112,17... | collective-permute-start | bytes 1474568 | tf_op jit(solution)/shard_map/ppermute | solution.py:132
  83.0 18.9 %collective-permute-start.12 = (bf16[320,768]{1,0:T(8,128)(2,1)}, bf16[320,768]{1,0:T(8,128)(2,1)}, u32[]{:S(2)}, u32[]{:S(2)}) collective-permute-start(bf16[320,768]{1,0:T(8,128)(2,1)} %broadcast_select_fusion.1.refs_17_), channel_id=1, source_target_pairs={{0,192},{16,208},{32,224},{48,240},{64,0},{80,16},{96,32},{112,48}... | collective-permute-start | bytes 1474568 | tf_op jit(solution)/shard_map/ppermute | solution.py:132
  84.4 0.8 copy-start.1
  91.0 19.0 %collective-permute-start.11 = (bf16[32,5120]{1,0:T(8,128)(2,1)}, bf16[32,5120]{1,0:T(8,128)(2,1)}, u32[]{:S(2)}, u32[]{:S(2)}) collective-permute-start(bf16[32,5120]{1,0:T(8,128)(2,1)} %gate.35.refs_1_), channel_id=1, source_target_pairs={{0,8},{1,9},{2,10},{3,11},{4,12},{5,13},{6,14},{7,15},{8,0},{9,1},... | collective-permute-start | bytes 983048 | tf_op jit(solution)/shard_map/ppermute | solution.py:132
  95.2 17.8 %collective-permute-start.18 = (bf16[320,768]{1,0:T(8,128)(2,1)}, bf16[320,768]{1,0:T(8,128)(2,1)}, u32[]{:S(2)}, u32[]{:S(2)}) collective-permute-start(bf16[320,768]{1,0:T(8,128)(2,1)} %broadcast_select_fusion.refs_21_), channel_id=1, source_target_pairs={{0,64},{16,80},{32,96},{48,112},{64,128},{80,144},{96,160},{112,17... | collective-permute-start | bytes 1474568 | tf_op jit(solution)/shard_map/ppermute | solution.py:132
  96.4 0.8 copy-start.2
  96.4 16.6 %collective-permute-start.17 = (bf16[320,768]{1,0:T(8,128)(2,1)}, bf16[320,768]{1,0:T(8,128)(2,1)S(1)}, u32[]{:S(2)}, u32[]{:S(2)}) collective-permute-start(bf16[320,768]{1,0:T(8,128)(2,1)} %broadcast_select_fusion.refs_21_), channel_id=1, source_target_pairs={{0,192},{16,208},{32,224},{48,240},{64,0},{80,16},{96,32},{112,48}... | collective-permute-start | bytes 1474568 | tf_op jit(solution)/shard_map/ppermute | solution.py:132
  101.9 16.5 %collective-permute-start.16 = (bf16[320,768]{1,0:T(8,128)(2,1)}, bf16[320,768]{1,0:T(8,128)(2,1)}, u32[]{:S(2)}, u32[]{:S(2)}) collective-permute-start(bf16[320,768]{1,0:T(8,128)(2,1)} %gate.38.refs_1_.refs_19_), channel_id=1, source_target_pairs={{0,192},{16,208},{32,224},{48,240},{64,0},{80,16},{96,32},{112,48}... | collective-permute-start | bytes 1474568 | tf_op jit(solution)/shard_map/ppermute | solution.py:132
  110.0 8.4 %collective-permute-start.15 = (bf16[32,5120]{1,0:T(8,128)(2,1)}, bf16[32,5120]{1,0:T(8,128)(2,1)}, u32[]{:S(2)}, u32[]{:S(2)}) collective-permute-start(bf16[32,5120]{1,0:T(8,128)(2,1)} %gate.39.refs_1_), channel_id=1, source_target_pairs={{0,1},{1,0},{2,3},{3,2},{4,5},{5,4},{6,7},{7,6},{8,9},{9,8},{10,11... | collective-permute-start | bytes 983048 | tf_op jit(solution)/shard_map/ppermute | solution.py:132
  110.0 11.0 %collective-permute-start.20 = (bf16[32,5120]{1,0:T(8,128)(2,1)}, bf16[32,5120]{1,0:T(8,128)(2,1)}, u32[]{:S(2)}, u32[]{:S(2)}) collective-permute-start(bf16[32,5120]{1,0:T(8,128)(2,1)} %gate.39.refs_1_), channel_id=1, source_target_pairs={{0,6},{1,7},{2,0},{3,1},{4,2},{5,3},{6,4},{7,5},{8,14},{9,15},{10,... | collective-permute-start | bytes 983048 | tf_op jit(solution)/shard_map/ppermute | solution.py:132
  113.0 13.6 %collective-permute-start.24 = (bf16[320,768]{1,0:T(8,128)(2,1)}, bf16[320,768]{1,0:T(8,128)(2,1)S(1)}, u32[]{:S(2)}, u32[]{:S(2)}) collective-permute-start(bf16[320,768]{1,0:T(8,128)(2,1)} %gate.40.refs_1_.refs_22_), channel_id=1, source_target_pairs={{0,64},{16,80},{32,96},{48,112},{64,128},{80,144},{96,160},{112,17... | collective-permute-start | bytes 1474568 | tf_op jit(solution)/shard_map/ppermute | solution.py:132
  113.0 11.6 %collective-permute-start.19 = (bf16[32,5120]{1,0:T(8,128)(2,1)}, bf16[32,5120]{1,0:T(8,128)(2,1)}, u32[]{:S(2)}, u32[]{:S(2)}) collective-permute-start(bf16[32,5120]{1,0:T(8,128)(2,1)} %gate.39.refs_1_), channel_id=1, source_target_pairs={{0,2},{1,3},{2,4},{3,5},{4,6},{5,7},{6,0},{7,1},{8,10},{9,11},{10,... | collective-permute-start | bytes 983048 | tf_op jit(solution)/shard_map/ppermute | solution.py:132
  121.0 10.9 %collective-permute-start.23 = (bf16[32,5120]{1,0:T(8,128)(2,1)}, bf16[32,5120]{1,0:T(8,128)(2,1)S(1)}, u32[]{:S(2)}, u32[]{:S(2)}) collective-permute-start(bf16[32,5120]{1,0:T(8,128)(2,1)} %gate.44.refs_1_.refs_5_), channel_id=1, source_target_pairs={{0,6},{1,7},{2,0},{3,1},{4,2},{5,3},{6,4},{7,5},{8,14},{9,15},{10,... | collective-permute-start | bytes 983048 | tf_op jit(solution)/shard_map/ppermute | solution.py:132
  124.6 9.2 %collective-permute-start.22 = (bf16[32,5120]{1,0:T(8,128)(2,1)}, bf16[32,5120]{1,0:T(8,128)(2,1)}, u32[]{:S(2)}, u32[]{:S(2)}) collective-permute-start(bf16[32,5120]{1,0:T(8,128)(2,1)} %gate.44.refs_1_.refs_5_), channel_id=1, source_target_pairs={{0,1},{1,0},{2,3},{3,2},{4,5},{5,4},{6,7},{7,6},{8,9},{9,8},{10,11... | collective-permute-start | bytes 983048 | tf_op jit(solution)/shard_map/ppermute | solution.py:132
  124.7 9.2 %collective-permute-start.21 = (bf16[32,5120]{1,0:T(8,128)(2,1)}, bf16[32,5120]{1,0:T(8,128)(2,1)}, u32[]{:S(2)}, u32[]{:S(2)}) collective-permute-start(bf16[32,5120]{1,0:T(8,128)(2,1)} %gate.45.refs_1_.refs_3_), channel_id=1, source_target_pairs={{0,1},{1,0},{2,3},{3,2},{4,5},{5,4},{6,7},{7,6},{8,9},{9,8},{10,11... | collective-permute-start | bytes 983048 | tf_op jit(solution)/shard_map/ppermute | solution.py:132
  126.6 0.8 copy-start.5
  132.6 1.8 collective-permute-start.25
  (4 other events, 3.1 us)
Sparse Core Ops, SparseCore 0:
  11.4 53.0 all-gather.2
  66.3 39.2 all-gather.4
